TPU v7x, 256 devices: a whole 4x4x8 slice. The times are simulated.
256 devices in a mesh: dp: 32 (over y_hi, z, core), expert: 8 (over x, y_lo).
Axes of the slice: x: 4, y: 4 (y_hi: 2, y_lo: 2; y = y_hi * 2 + y_lo), z: 8, core: 2. Of those that a mesh axis runs over, the one named last changes fastest.
Arguments:
- tokens: float32 [32768, 3584], P(('dp', 'expert')), may hold values from -24 to 24
- cotangent: float32 [32768, 3584], P(('dp', 'expert')), may hold values from -6 to 6
- routes: int32 [32768, 2], P(('dp', 'expert')), may hold values from 0 to 7, all different within a row; in each aligned block of 128 rows (0 to 127, 128 to 255, ...) at most 40 rows name the same one
- gates: float32 [32768, 2], P(('dp', 'expert')), may hold values from 0.1 to 1
- w_gate: float32 [8, 3584, 128], P('expert', 'dp'), may hold values from -0.09375 to 0.09375
- w_up: float32 [8, 3584, 128], P('expert', 'dp'), may hold values from -0.09375 to 0.09375
- w_down: float32 [8, 3584, 128], P('expert', 'dp'), may hold values from -0.5 to 0.5
Outputs:
- grad_tokens: float32 [32768, 3584], P(('dp', 'expert'))
- grad_gate: float32 [8, 3584, 128], P('expert', 'dp')
- grad_up: float32 [8, 3584, 128], P('expert', 'dp')
- grad_down: float32 [8, 3584, 128], P('expert', 'dp')
Inputs may be any that keep to these rules, and one draw needn't show every extreme that they name: Within the rows of one device (aligned blocks of 128 rows), no expert is named by more than 40 routes, a bound that some block reaches; the 2 experts of a row differ.
All inputs are finite; a program needn't handle non-finite values.
Results may differ from a plain program's by a relative error of at most 0.0003.
Values sent between devices are 32-bit elements; how exact they have to be, the bound alone decides.
A program may use at most 128 MiB of HBM per device.

v0:
```python
import jax
import jax.numpy as jnp
from jax import lax
from jax.sharding import PartitionSpec as P

highest = lax.Precision.HIGHEST


def silu_parts(pre_act):
    sigmoid_val = jax.nn.sigmoid(pre_act)
    return (pre_act * sigmoid_val, sigmoid_val * (1.0 + pre_act * (1.0 - sigmoid_val)))


def contract_rows(left_side, right_side):
    return lax.dot_general(left_side, right_side, (((0,), (0,)), ((), ())), precision=highest)


def contract_columns(left_side, right_side):
    return lax.dot_general(left_side, right_side, (((1,), (1,)), ((), ())), precision=highest)


def local(tokens, cotangent, routes, gates, w_gate, w_up, w_down):
    row_count, model_width = tokens.shape
    top_count = routes.shape[1]
    experts_here = lax.axis_size("expert")
    capacity = min(row_count, row_count * top_count * 5 // (4 * experts_here))
    slot_total = experts_here * capacity
    route_total = row_count * top_count
    flat_expert = routes.reshape(-1)
    onehot = (flat_expert[:, None] == jnp.arange(experts_here, dtype=jnp.int32)[None, :]).astype(
        jnp.int32
    )
    route_rank = jnp.sum((jnp.cumsum(onehot, axis=0) - 1) * onehot, axis=1)
    slot_index = flat_expert * capacity + route_rank
    slot_match = slot_index[None, :] == jnp.arange(slot_total, dtype=jnp.int32)[:, None]
    filled = jnp.any(slot_match, axis=1)[:, None]
    source = jnp.sum(
        jnp.where(slot_match, jnp.arange(route_total, dtype=jnp.int32)[None, :], 0), axis=1
    )
    token_index = source // top_count
    sent_rows = jnp.where(filled, tokens[token_index], 0.0).reshape(
        experts_here, capacity, model_width
    )
    sent_grads = jnp.where(filled, cotangent[token_index] * gates.reshape(-1)[source][:, None], 0.0)
    sent_grads = sent_grads.reshape(experts_here, capacity, model_width)
    got_rows, got_grads = (
        lax.all_to_all(sent_rows, "expert", split_axis=0, concat_axis=0, tiled=True),
        lax.all_to_all(sent_grads, "expert", split_axis=0, concat_axis=0, tiled=True),
    )
    got_rows = got_rows.reshape(slot_total, model_width)
    got_grads = got_grads.reshape(slot_total, model_width)
    gate_shard = w_gate[0]
    up_shard = w_up[0]
    down_shard = w_down[0]
    shard_rows, hidden_width = gate_shard.shape
    gate_full, up_full, down_full = (
        lax.all_gather(gate_shard, "dp", axis=0, tiled=True),
        lax.all_gather(up_shard, "dp", axis=0, tiled=True),
        lax.all_gather(down_shard, "dp", axis=0, tiled=True),
    )
    pre_gate = jnp.dot(got_rows, gate_full, precision=highest)
    pre_up = jnp.dot(got_rows, up_full, precision=highest)
    back_hidden = jnp.dot(got_grads, down_full, precision=highest)
    activated, slopes = silu_parts(pre_gate)
    hidden = activated * pre_up
    grad_gate_pre = back_hidden * pre_up * slopes
    grad_up_pre = back_hidden * activated
    row_grads = contract_columns(grad_gate_pre, gate_full) + contract_columns(grad_up_pre, up_full)
    returned = lax.all_to_all(
        row_grads.reshape(experts_here, capacity, model_width),
        "expert",
        split_axis=0,
        concat_axis=0,
        tiled=True,
    )
    picked_back = returned.reshape(slot_total, model_width)[slot_index]
    grad_tokens = picked_back.reshape(row_count, top_count, model_width).sum(axis=1)
    both_pre = jnp.concatenate([grad_gate_pre, grad_up_pre], axis=1)
    shares = lax.psum_scatter(
        jnp.concatenate(
            [contract_rows(got_rows, both_pre), contract_rows(got_grads, hidden)], axis=1
        ),
        "dp",
        scatter_dimension=0,
        tiled=True,
    )
    grad_gate = shares[:, :hidden_width]
    grad_up = shares[:, hidden_width : 2 * hidden_width]
    grad_down = shares[:, 2 * hidden_width :]
    return (grad_tokens, grad_gate[None], grad_up[None], grad_down[None])


def solution(mesh):
    placed = (
        P(("dp", "expert"), None),
        P(("dp", "expert"), None),
        P(("dp", "expert"), None),
        P(("dp", "expert"), None),
        P("expert", "dp", None),
        P("expert", "dp", None),
        P("expert", "dp", None),
    )
    return jax.shard_map(
        local,
        mesh=mesh,
        in_specs=placed,
        out_specs=(
            P(("dp", "expert"), None),
            P("expert", "dp", None),
            P("expert", "dp", None),
            P("expert", "dp", None),
        ),
        check_vma=False,
    )
```

profile of v0, /device:TPU:32, one launch (start us, length us, event | category | flops | bytes accessed | tf_op | source)
XLA Modules:
  0.0 476.1 jit_solution(10594014483236752098)
XLA Ops:
  7.2 0.0 copy-start
  7.2 0.0 all-gather.11.cloned.1.call-start
  7.2 0.7 all-gather.11.cloned.1.call-update
  7.9 0.8 copy.28
  8.7 0.1 eq.39
  8.9 0.1 reshape.172
  9.0 0.6 reduce-window.6
  9.6 0.2 slice_reduce_fusion
  9.8 0.1 fusion.19
  9.9 0.2 select_reduce_fusion
  10.1 0.0 copy-done
  10.2 4.1 gather_fusion
  14.2 0.0 copy-start.5
  14.2 8.8 %gather_fusion.2 = f32[320,3584]{1,0:T(8,128)} fusion(f32[128,3584]{1,0:T(8,128)} %param.7, s32[1024]{0:T(1024)S(1)} %get-tuple-element.30), kind=kCustom, calls=%fused_computation.2 | custom fusion | bytes 9176320 | tf_op jit(solution)/shard_map/gather | solution.py:41
  23.0 0.0 copy-done.5
  23.0 0.1 copy.30
  23.1 0.1 reshape.174
  23.3 2.5 gather_fusion.1
  25.7 0.1 mul.62
  25.8 0.2 fusion.13
  26.0 0.1 broadcast_in_dim.49
  26.0 8.7 %multiply_select_fusion = (f32[8,40,3584]{2,1,0:T(8,128)}, f32[8,40,3584]{2,1,0:T(8,128)}) fusion(f32[8,40,3584]{2,1,0:T(8,128)} %bitcast.41, f32[8,40]{1,0:T(8,128)S(1)} %mul.62, pred[8,40]{1,0:T(8,128)(4,1)S(1)} %broadcast_in_dim.49, f32[8,40,3584]{2,1,0:T(8,128)} %bitcast.42), kind=kLoop, calls=%fused_computation.6 | loop fusion | flops 3440640 | bytes 18351680 | tf_op jit(solution)/shard_map/jit(_where)/select_n | solution.py:44
  34.7 5.3 %all-to-all-start.1 = ((f32[8,40,3584]{2,1,0:T(8,128)}), f32[8,40,3584]{2,1,0:T(8,128)}, u32[]{:S(2)}, u32[]{:S(2)}) async-start(f32[8,40,3584]{2,1,0:T(8,128)} %get-tuple-element.28), calls=%async_computation.1 | async-start | bytes 9175040 | tf_op jit(solution)/shard_map/all_to_all | solution.py:47
  40.0 0.0 all-gather.9.cloned.1.call-start
  40.1 0.7 all-gather.9.cloned.1.call-update
  40.8 64.2 %all-to-all-done.1 = f32[8,40,3584]{2,1,0:T(8,128)} async-done(((f32[8,40,3584]{2,1,0:T(8,128)}), f32[8,40,3584]{2,1,0:T(8,128)}, u32[]{:S(2)}, u32[]{:S(2)}) %all-to-all-start.1) | async-done | bytes 4587552 | tf_op jit(solution)/shard_map/all_to_all | solution.py:47
  104.9 4.6 all-to-all-start
  109.5 0.0 all-gather.7.cloned.1.call-start
  109.6 0.7 all-gather.7.cloned.1.call-update
  110.3 0.2 reduce-scatter.4.cloned.1.call-start
  110.5 0.0 all-gather.11.cloned.1.call-done
  110.5 6.2 %fusion.2 = f32[320,128]{1,0:T(8,128)S(1)} fusion(f32[320,3584]{1,0:T(8,128)} %bitcast.6, f32[1,3584,128]{2,1,0:T(8,128)} %all-gather.11.cloned.1.call-done), kind=kOutput, calls=%fused_computation.10 | convolution fusion | flops 1761607680 | bytes 6586368 | tf_op jit(solution)/shard_map/dot_general | solution.py:61
  116.7 104.0 %all-gather.9.cloned.1.call-done = f32[1,3584,128]{2,1,0:T(8,128)} async-done(((f32[1,112,128]{2,1,0:T(8,128)}), f32[1,3584,128]{2,1,0:T(8,128)}) %all-gather.9.cloned.1.call-update) | async-done | bytes 1835024 | tf_op jit(solution)/shard_map/all_gather | solution.py:58
  220.8 6.2 %fusion.5 = f32[320,128]{1,0:T(8,128)S(1)} fusion(f32[320,3584]{1,0:T(8,128)} %bitcast.6, f32[1,3584,128]{2,1,0:T(8,128)} %all-gather.9.cloned.1.call-done), kind=kOutput, calls=%fused_computation.13 | convolution fusion | flops 1761607680 | bytes 6586368 | tf_op jit(solution)/shard_map/dot_general | solution.py:62
  227.0 0.0 all-to-all-done
  227.0 5.6 %fusion.14 = f32[3584,128]{0,1:T(8,128)S(1)} fusion(f32[320,3584]{1,0:T(8,128)} %bitcast.3, f32[320,128]{1,0:T(8,128)S(1)} %fusion.5, f32[320,128]{1,0:T(8,128)S(1)} %fusion.2), kind=kOutput, calls=%fused_computation.24 | convolution fusion | flops 1761812480 | bytes 6750208 | tf_op jit(solution)/shard_map/dot_general | solution.py:15
  232.6 66.9 %all-gather.7.cloned.1.call-done = f32[1,3584,128]{2,1,0:T(8,128)} async-done(((f32[1,112,128]{2,1,0:T(8,128)}), f32[1,3584,128]{2,1,0:T(8,128)}) %all-gather.7.cloned.1.call-update) | async-done | bytes 1835024 | tf_op jit(solution)/shard_map/all_gather | solution.py:59
  299.4 6.2 %fusion.18 = (f32[320,128]{1,0:T(8,128)S(1)}, f32[320,128]{1,0:T(8,128)S(1)}) fusion(f32[320,128]{1,0:T(8,128)S(1)} %fusion.2, f32[320,128]{1,0:T(8,128)S(1)} %fusion.5, f32[320,3584]{1,0:T(8,128)} %bitcast.3, f32[1,3584,128]{2,1,0:T(8,128)} %all-gather.7.cloned.1.call-done), kind=kOutput, calls=%fused_computation.29 | convolution fusion | flops 1762058240 | bytes 7077888 | tf_op jit(solution)/shard_map/dot_general | solution.py:63
  305.6 8.1 %fusion.9 = f32[3584,256]{0,1:T(8,128)S(1)} fusion(f32[320,3584]{1,0:T(8,128)} %bitcast.6, f32[320,128]{1,0:T(8,128)S(1)} %get-tuple-element.22, f32[320,128]{1,0:T(8,128)S(1)} %get-tuple-element.23), kind=kOutput, calls=%fused_computation.17 | convolution fusion | flops 3523297280 | bytes 8585216 | tf_op jit(solution)/shard_map/dot_general | solution.py:15
  313.7 2.8 pad_maximum_fusion
  316.5 6.1 %copy.35 = f32[3584,384]{1,0:T(8,128)} copy(f32[3584,384]{0,1:T(8,128)} %pad_maximum_fusion) | data formatting | bytes 11010048
  322.6 0.0 copy-start.2
  322.6 0.0 reduce-scatter.4.cloned.1.call-update
  322.6 1.5 copy-done.2
  324.1 3.9 fusion
  328.0 0.0 copy-done.3
  328.0 5.5 %convolution_add_fusion = f32[320,3584]{1,0:T(8,128)} fusion(f32[320,3584]{1,0:T(8,128)S(1)} %fusion, f32[320,128]{1,0:T(8,128)S(1)} %get-tuple-element.22, f32[1,3584,128]{2,1,0:T(8,128)S(1)} %copy-done.3), kind=kOutput, calls=%fused_computation.4 | convolution fusion | flops 1762754560 | bytes 11173888 | tf_op jit(solution)/shard_map/dot_general | solution.py:19
  333.5 4.8 %all-to-all-start.2 = ((f32[8,40,3584]{2,1,0:T(8,128)}), f32[8,40,3584]{2,1,0:T(8,128)}, u32[]{:S(2)}, u32[]{:S(2)}) async-start(f32[8,40,3584]{2,1,0:T(8,128)} %bitcast.40), calls=%async_computation.2 | async-start | bytes 9175040 | tf_op jit(solution)/shard_map/all_to_all | solution.py:69
  338.3 0.0 copy-done.4
  338.3 0.1 copy.31
  338.4 0.1 mul.73
  338.6 65.2 %all-to-all-done.2 = f32[8,40,3584]{2,1,0:T(8,128)} async-done(((f32[8,40,3584]{2,1,0:T(8,128)}), f32[8,40,3584]{2,1,0:T(8,128)}, u32[]{:S(2)}, u32[]{:S(2)}) %all-to-all-start.2) | async-done | bytes 4587552 | tf_op jit(solution)/shard_map/all_to_all | solution.py:69
  403.8 7.6 %gather_fusion.3 = f32[256,3584]{1,0:T(8,128)} fusion(f32[320,3584]{1,0:T(8,128)} %bitcast.10, s32[1024]{0:T(1024)S(1)} %pad_clamp_fusion), kind=kCustom, calls=%fused_computation.3 | custom fusion | bytes 7341056 | tf_op jit(solution)/shard_map/gather | solution.py:76
  411.4 5.9 %reshape.179 = f32[128,2,3584]{2,1,0:T(2,128)} reshape(f32[256,3584]{1,0:T(8,128)} %gather_fusion.3) | data formatting | bytes 7340032 | tf_op jit(solution)/shard_map/reshape | solution.py:77
  417.3 7.7 %reduce_sum.35 = f32[128,3584]{1,0:T(8,128)} reduce(f32[128,2,3584]{2,1,0:T(2,128)} %reshape.179, f32[]{:T(128)} %constant.34.clone.1), dimensions={1}, to_apply=%region_5.6 | reduce | flops 458752 | bytes 5505028 | tf_op jit(solution)/shard_map/reduce_sum | solution.py:77
  425.0 41.3 %reduce-scatter.4.cloned.1.call-done = f32[112,384]{1,0:T(8,128)} async-done(((f32[3584,384]{1,0:T(8,128)}), f32[112,384]{1,0:T(8,128)}) %reduce-scatter.4.cloned.1.call-update) | async-done | bytes 172048
  466.2 0.9 fusion.25
  467.1 0.1 copy.37
  467.2 0.7 copy.32
  467.9 0.1 copy.38
  468.0 0.7 copy.33
  468.7 0.1 copy.39
  468.8 0.7 copy.34
  469.6 0.0 copy-done.1
  (12 shorter events, 0.1 us)
Async XLA Ops:
  7.2 3.0 copy-start
  7.2 103.3 %all-gather.11.cloned.1.call-start = ((), (), s32[]{:S(2)}) async-start(), calls=%async_computation.6 | async-start | bytes 1892352 | tf_op jit(solution)/shard_map/all_gather | solution.py:57
  14.2 8.8 %copy-start.5 = (f32[128,2]{0,1:T(2,128)S(1)}, f32[128,2]{0,1:T(2,128)}, u32[]{:S(2)}) copy-start(f32[128,2]{0,1:T(2,128)} %param.10) | copy-start | bytes 3076
  34.7 70.2 %all-to-all-start.1 = ((f32[8,40,3584]{2,1,0:T(8,128)}), f32[8,40,3584]{2,1,0:T(8,128)}, u32[]{:S(2)}, u32[]{:S(2)}) async-start(f32[8,40,3584]{2,1,0:T(8,128)} %get-tuple-element.28), calls=%async_computation.1 | async-start | bytes 9175040 | tf_op jit(solution)/shard_map/all_to_all | solution.py:47
  40.0 180.8 %all-gather.9.cloned.1.call-start = ((), (), s32[]{:S(2)}) async-start(), calls=%async_computation.5 | async-start | bytes 1892352 | tf_op jit(solution)/shard_map/all_gather | solution.py:58
  104.9 122.0 %all-to-all-start = ((f32[8,40,3584]{2,1,0:T(8,128)}), f32[8,40,3584]{2,1,0:T(8,128)}, u32[]{:S(2)}, u32[]{:S(2)}) async-start(f32[8,40,3584]{2,1,0:T(8,128)} %get-tuple-element.27), calls=%async_computation | async-start | bytes 9175040 | tf_op jit(solution)/shard_map/all_to_all | solution.py:48
  109.5 189.9 %all-gather.7.cloned.1.call-start = ((), (), s32[]{:S(2)}) async-start(), calls=%async_computation.4 | async-start | bytes 1892352 | tf_op jit(solution)/shard_map/all_gather | solution.py:59
  110.3 355.9 %reduce-scatter.4.cloned.1.call-start = ((), (), s32[]{:S(2)}) async-start(), calls=%async_computation.7 | async-start | bytes 5677056
  322.6 1.5 copy-start.2
  324.1 3.9 copy-start.3
  333.5 4.8 %copy-start.4 = (s32[128,2]{0,1:T(2,128)S(1)}, s32[128,2]{0,1:T(2,128)}, u32[]{:S(2)}) copy-start(s32[128,2]{0,1:T(2,128)} %param.9) | copy-start | bytes 3076
  333.5 70.3 %all-to-all-start.2 = ((f32[8,40,3584]{2,1,0:T(8,128)}), f32[8,40,3584]{2,1,0:T(8,128)}, u32[]{:S(2)}, u32[]{:S(2)}) async-start(f32[8,40,3584]{2,1,0:T(8,128)} %bitcast.40), calls=%async_computation.2 | async-start | bytes 9175040 | tf_op jit(solution)/shard_map/all_to_all | solution.py:69
  411.4 58.1 %copy-start.1 = (f32[128,3584]{1,0:T(8,128)S(1)}, f32[128,3584]{1,0:T(8,128)}, u32[]{:S(2)}) copy-start(f32[128,3584]{1,0:T(8,128)} %param.8) | copy-start | bytes 5505028
Sparse Core Ops, SparseCore 0:
  10.8 90.5 all-gather.10
  104.1 116.6 all-gather.8
  223.6 75.8 all-gather.6
  322.8 143.4 reduce-scatter.3
where the time goes:
time: 478 us; the launch traced here: 476 us
  waiting for transfers between devices  344 us (72%)
  local copies, waits for them, and re-layouts  41.6 us (9%)
  matrix products  41.5 us (9%)
  other arithmetic  20.2 us (4%)
  starting transfers between devices  15 us (3%)
  between operations  14 us (3%)
    all_gather x1, waiting for transfers between devices, local(): lax.all_gather(up_shard, 'dp', axis=0, tiled=True)  104 us
    all_gather x1, waiting for transfers between devices, local(): lax.all_gather(down_shard, 'dp', axis=0, tiled=True)  66.9 us
    all_to_all x1, waiting for transfers between devices, local(): lax.all_to_all(row_grads.reshape(experts_here, capacity, model_width), 'e...  65.2 us
    all_to_all x1, waiting for transfers between devices, local(): lax.all_to_all(sent_rows, 'expert', split_axis=0, concat_axis=0, tiled=True)  64.2 us
    unnamed x5, waiting for transfers between devices  43.3 us
    dot_general x2, matrix products, contract_rows(): lax.dot_general(left_side, right_side, (((0,), (0,)), ((), ())), precisio...  13.6 us
    unnamed x21, local copies, waits for them, and re-layouts  10.9 us
  transfers between devices with their start and end apart: 7, of which 5 were waited for; matrix products, arithmetic and copies ran while one was open for 16% of the time, Pallas kernels for 0%

commit v1 on v0

v1 whole, which is shorter than its diff:
```python
import jax
import jax.numpy as jnp
from jax import lax
from jax.experimental import pallas as pl
from jax.experimental.pallas import tpu as pltpu
from jax.sharding import PartitionSpec as P

MESH = pl.DeviceIdType.MESH
VMEM_LIMIT = 62 * 2**20
ROWS = 112
TOK = 128
F32 = jnp.float32
BF16 = jnp.bfloat16
NN = (((1,), (0,)), ((), ()))
NT = (((1,), (1,)), ((), ()))


def coords():
    dp = lax.axis_index("dp")
    e = lax.axis_index("expert")
    return e // 2, (dp // 16) * 2 + e % 2, (dp // 2) % 8, dp % 2


def dev(x, y, z, c):
    x, y, z, c = (x + 4) % 4, (y + 4) % 4, (z + 8) % 8, c % 2
    return ((y // 2) * 8 + z) * 2 + c, x * 2 + y % 2


def remote(src, dst, ss, rs, to):
    return pltpu.make_async_remote_copy(
        src_ref=src, dst_ref=dst, send_sem=ss, recv_sem=rs, device_id=to, device_id_type=MESH
    )


def greet(peers):
    bar = pltpu.get_barrier_semaphore()
    for p in peers:
        pl.semaphore_signal(bar, 1, device_id=p, device_id_type=MESH)
    pl.semaphore_wait(bar, len(peers))


def split(v):
    hi = v.astype(BF16)
    return hi, (v - hi.astype(F32)).astype(BF16)


def dot3(a, b, dims):
    def d(p, q):
        return lax.dot_general(p, q, dims, preferred_element_type=F32)

    return d(a[0], b[0]) + d(a[0], b[1]) + d(a[1], b[0])


PIECES = []
for j in range(28):
    r = j * 128
    found = []
    while r < j * 128 + 128:
        shard = r // ROWS
        stop = min((shard + 1) * ROWS, j * 128 + 128)
        yh, zz, cc = shard // 16, (shard // 2) % 8, shard % 2
        member = (yh * 2 + zz % 2) * 2 + cc
        found.append((member, (zz // 2) * ROWS + r - shard * ROWS, r - j * 128, stop - r))
        r = stop
    PIECES.append(found)

OTHERS = [(dc, dy) for dy in (2, 1, 3, 0) for dc in (0, 1) if (dc, dy) != (0, 0)]


def kernel(
    tok, cot, route, gate, w0, w1, w2, out, gout,
    xs, xg, wg, wsp, tsp, ttsp, infot, part, buf, got, ga, gd, gx, xh, xf, zh, z1, z2, z3,
    s_l, ss_x, rs_x, ss_p, rs_p, ss_z, rs_z, ss_r, rs_r,
    ss_a, rs_a, ss_b, rs_b, ss_c, rs_c, ss_d, rs_d,
    ss_t, rs_t, ss_q, rs_q, ss_y, rs_y, ss_s, rs_s,
):
    x, y, z, c = coords()
    yl = y % 2
    good = (z % 2) == yl
    bad = jnp.logical_not(good)
    me = y * 2 + c
    zi = z // 2
    zp, zm = dev(x, y, z + 1, c), dev(x, y, z - 1, c)
    xp, xm = dev(x + 1, y, z, c), dev(x - 1, y, z, c)
    partner = dev(x, (y // 2) * 2 + 1 - yl, z, c)
    sib = dev(x, y, z, 1 - c)
    greet([dev(x, y + dy, z, c + dc) for dc, dy in OTHERS] + [zp, zm, xp, xm])

    def rows(b):
        return pl.ds(pl.multiple_of(((b + 4) % 4) * ROWS, 16), ROWS)

    def cols(xx):
        return pl.ds(pl.multiple_of(((xx + 4) % 4) * 256, 256), 256)

    def hcols(xx, h):
        return pl.ds(pl.multiple_of(((xx + 4) % 4) * 256 + h * 128, 128), 128)

    def blk(xx, b):
        return wg.at[:, rows(b), cols(xx)]

    def half(xx, b, h):
        return wg.at[:, rows(b), hcols(xx, h)]

    ws = (w0, w1, w2)
    local = [pltpu.make_async_copy(ws[k], wg.at[k, rows(zi), hcols(x, yl)], s_l.at[k]) for k in range(3)]
    shift = [
        remote(ws[k], wg.at[k, rows(zi), hcols(x, yl)], ss_p.at[k], rs_p.at[k], partner) for k in range(3)
    ]

    @pl.when(good)
    def _():
        for cp in local:
            cp.start()

    @pl.when(bad)
    def _():
        for cp in shift:
            cp.start()

    lane = lax.broadcasted_iota(jnp.int32, (TOK, TOK), 1)
    facts = jnp.where(
        lane == 0,
        route[:, 0:1].astype(F32),
        jnp.where(
            lane == 1,
            route[:, 1:2].astype(F32),
            jnp.where(lane == 2, gate[:, 0:1], jnp.where(lane == 3, gate[:, 1:2], 0.0)),
        ),
    )
    facts = facts.T[0:8]
    for m in range(8):
        xs[m, 896:904, :] = facts
    for j in range(28):
        for a, ref in ((0, tok), (1, cot)):
            t = ref[:, j * 128 : (j + 1) * 128].T
            for m, to, frm, n in PIECES[j]:
                xs[m, a * 448 + to : a * 448 + to + n, :] = t[frm : frm + n]
    keep = pltpu.make_async_copy(xs.at[me], xg.at[me], s_l.at[3])
    keep.start()
    tokens_out = []
    for i, (dc, dy) in enumerate(OTHERS):
        y2, c2 = (y + dy) % 4, (c + dc) % 2
        cp = remote(xs.at[y2 * 2 + c2], xg.at[me], ss_x.at[i], rs_x.at[i], dev(x, y2, z, c2))
        cp.start()
        tokens_out.append(cp)

    lo = (z - 1 - yl + 8) // 2
    hi = lo + 1
    b0 = jnp.where(good, zi, lo)
    b1 = jnp.where(good, zi - 1, hi)
    b2 = jnp.where(good, zi + 1, lo - 1)
    b3 = jnp.where(good, zi + 2, hi + 1)

    def zcp(i, ref, to):
        return remote(ref, ref, ss_z.at[i], rs_z.at[i], to)

    def xcp(s, i, ref):
        return remote(ref, ref, ss_r.at[s, i], rs_r.at[s, i], xp if i % 2 == 0 else xm)

    def start_x(s, b):
        xcp(s, 0, blk(x, b)).start()
        xcp(s, 1, blk(x, b)).start()

    def forward_x(s, b):
        xcp(s, 0, blk(x - 1, b)).wait_recv()
        xcp(s, 2, half(x - 1, b, 0)).start()
        xcp(s, 1, blk(x + 1, b)).wait_recv()
        xcp(s, 3, half(x + 1, b, 1)).start()

    def finish_x(s, b):
        xcp(s, 2, half(x - 2, b, 0)).wait_recv()
        xcp(s, 3, half(x + 2, b, 1)).wait_recv()
        for i in range(4):
            (xcp(s, i, blk(x, b)) if i < 2 else xcp(s, i, half(x, b, 0))).wait_send()

    @pl.when(good)
    def _():
        for k in range(3):
            local[k].wait()
            remote(ws[k], wg.at[k, rows(zi), hcols(x, 1 - yl)], ss_p.at[k], rs_p.at[k], partner).wait_recv()
        zcp(0, blk(x, b0), zp).start()
        zcp(2, blk(x, b0), zm).start()
        start_x(0, b0)

    @pl.when(bad)
    def _():
        zcp(0, blk(x, b0), zp).wait_recv()
        zcp(0, blk(x, b0), zp).start()
        start_x(0, b0)
        zcp(2, blk(x, b1), zm).wait_recv()
        zcp(2, blk(x, b1), zm).start()
        start_x(1, b1)

    forward_x(0, b0)

    @pl.when(good)
    def _():
        zcp(0, blk(x, b1), zp).wait_recv()
        zcp(1, blk(x, b1), zp).start()
        start_x(1, b1)
        zcp(2, blk(x, b2), zm).wait_recv()
        zcp(3, blk(x, b2), zm).start()
        start_x(2, b2)

    forward_x(1, b1)

    @pl.when(bad)
    def _():
        zcp(1, blk(x, b2), zp).wait_recv()
        zcp(1, half(x, b2, 0), zp).start()
        start_x(2, b2)
        zcp(3, blk(x, b3), zm).wait_recv()
        zcp(3, half(x, b3, 1), zm).start()
        start_x(3, b3)

    forward_x(2, b2)

    @pl.when(good)
    def _():
        zcp(1, half(x, b3, 0), zp).wait_recv()
        zcp(3, half(x, b3, 1), zm).wait_recv()
        start_x(3, b3)

    forward_x(3, b3)
    for s, b in enumerate((b0, b1, b2, b3)):
        finish_x(s, b)
    zcp(0, blk(x, b0), zp).wait_send()
    zcp(2, blk(x, b0), zm).wait_send()

    @pl.when(good)
    def _():
        zcp(1, blk(x, b1), zp).wait_send()
        zcp(3, blk(x, b1), zm).wait_send()

    @pl.when(bad)
    def _():
        zcp(1, half(x, b1, 0), zp).wait_send()
        zcp(3, half(x, b1, 1), zm).wait_send()
        for cp in shift:
            cp.wait_send()

    def split_w(i, _):
        r = pl.ds(pl.multiple_of(i * 32, 32), 32)
        for k in range(3):
            h, l = split(wg[k, r, :])
            wsp[0, k, r, :] = h
            wsp[1, k, r, :] = l
        return 0

    lax.fori_loop(0, 14, split_w, 0)

    def member_rows(y2, c2):
        return pl.ds(pl.multiple_of(y2 * 256 + c2 * 128, 128), 128)

    def prepare(y2):
        for c2 in range(2):
            m = y2 * 2 + c2
            infot[m, :, 0:8] = xg[m, 896:904, :].T
            for a in range(2):
                v = xg[m, a * 448 : (a + 1) * 448, :]
                h, l = split(v)
                ttsp[0, a, :, member_rows(y2, c2)] = h
                ttsp[1, a, :, member_rows(y2, c2)] = l
                h, l = split(v.T)
                tsp[0, a, c2 * 128 : (c2 + 1) * 128, :] = h
                tsp[1, a, c2 * 128 : (c2 + 1) * 128, :] = l

    def forward(y2):
        r = [
            jnp.concatenate([infot[y2 * 2, :, k : k + 1], infot[y2 * 2 + 1, :, k : k + 1]], axis=0)
            for k in range(2)
        ]
        for kind in range(3):
            a = 1 if kind == 2 else 0
            t = tsp[0, a], tsp[1, a]
            sel = [jnp.zeros((256, 128), F32)] * 2
            for q in range(4):
                cs = slice(q * 256, (q + 1) * 256)
                res = dot3(t, (wsp[0, kind, :, cs], wsp[1, kind, :, cs]), NN)
                for e in range(2):
                    for k in range(2):
                        sel[k] = jnp.where(r[k] == float(q * 2 + e), res[:, e * 128 : (e + 1) * 128], sel[k])
            for k in range(2):
                base = (k * 3 + kind) * 128
                part[y2, 0, :, base : base + 128] = sel[k][0:128]
                part[y2, 1, :, base : base + 128] = sel[k][128:256]

    STEPS = (2, 1, 3, 0)

    def first(i):
        y2 = (y + STEPS[i]) % 4
        return remote(part.at[y2, 1 - c], buf.at[y2], ss_a.at[i], rs_a.at[i], sib)

    def second(i):
        y2 = (y + STEPS[i]) % 4
        return remote(buf.at[y2], got.at[i], ss_b.at[i], rs_b.at[i], dev(x, y2, z, c))

    def merge(i):
        y2 = (y + STEPS[i]) % 4
        first(i).wait_recv()
        buf[y2] = buf[y2] + part[y2, c]
        if i < 3:
            second(i).start()

    keep.wait()
    for i in range(4):
        y2 = (y + STEPS[i]) % 4
        for n, (dc, dy) in enumerate(OTHERS):
            if (4 - dy) % 4 == STEPS[i]:
                tokens_out[n].wait_recv()
        prepare(y2)
        forward(y2)
        first(i).start()
        if i:
            merge(i - 1)
    merge(3)
    total = buf[y]
    for i in range(3):
        second(i).wait_recv()
        total = total + got[i]

    for k in range(2):
        g = gate[:, k : k + 1]
        base = k * 384
        pre_gate = total[:, base : base + 128]
        pre_up = total[:, base + 128 : base + 256]
        back = total[:, base + 256 : base + 384] * g
        s = jax.nn.sigmoid(pre_gate)
        activated = pre_gate * s
        slopes = s * (1.0 + pre_gate * (1.0 - s))
        ga[y, c, :, base : base + 128] = back * pre_up * slopes
        ga[y, c, :, base + 128 : base + 256] = back * activated
        ga[y, c, :, base + 256 : base + 384] = activated * pre_up * g

    def spread(i):
        return remote(ga.at[y, c], ga.at[y, c], ss_c.at[i], rs_c.at[i], dev(x, y + STEPS[i], z, c))

    def pass_on(i, y2):
        return remote(ga.at[y2, c], ga.at[y2, c], ss_d.at[i], rs_d.at[i], sib)

    def expand(y2, c2):
        m = y2 * 2 + c2
        r0, r1 = infot[m, :, 0:1], infot[m, :, 1:2]
        for kind in range(3):
            g0 = ga[y2, c2, :, kind * 128 : (kind + 1) * 128]
            g1 = ga[y2, c2, :, (3 + kind) * 128 : (4 + kind) * 128]
            for e in range(8):
                v = jnp.where(r0 == float(e), g0, jnp.where(r1 == float(e), g1, 0.0))
                h, l = split(v)
                gd[0, kind, member_rows(y2, c2), e * 128 : (e + 1) * 128] = h
                gd[1, kind, member_rows(y2, c2), e * 128 : (e + 1) * 128] = l

    for i in range(3):
        spread(i).start()
    pass_on(3, y).start()
    expand(y, c)
    for i in (1, 2, 0):
        y2 = (y - STEPS[i] + 4) % 4
        remote(ga.at[y2, c], ga.at[y2, c], ss_c.at[i], rs_c.at[i], dev(x, y2, z, c)).wait_recv()
        pass_on(i, y2).start()
        expand(y2, c)
    for i in (3, 1, 2, 0):
        y2 = (y - STEPS[i] + 4) % 4
        remote(ga.at[y2, 1 - c], ga.at[y2, 1 - c], ss_d.at[i], rs_d.at[i], sib).wait_recv()
        expand(y2, 1 - c)
    for i in range(4):
        first(i).wait_send()
        pass_on(i, y).wait_send()
    for i in range(3):
        second(i).wait_send()
        spread(i).wait_send()
    for cp in tokens_out:
        cp.wait_send()

    def weight_grad(xx):
        for kind in range(3):
            a = 1 if kind == 2 else 0
            wg[kind, :, cols(xx)] = dot3(
                (ttsp[0, a], ttsp[1, a]), (gd[0, kind, :, cols(xx)], gd[1, kind, :, cols(xx)]), NN
            )

    o = [jnp.where(good, p, q) for p, q in ((zi + 2, hi + 1), (zi + 1, lo - 1), (zi - 1, hi), (zi, lo))]

    def shalf(s, h):
        return remote(
            half(x + 2, o[s], h), xh.at[s, h], ss_t.at[s, h], rs_t.at[s, h], xp if h == 0 else xm
        )

    def sfull(s, h):
        return remote(
            blk(x + 1 - 2 * h, o[s]), xf.at[s, h], ss_q.at[s, h], rs_q.at[s, h], xp if h == 0 else xm
        )

    weight_grad(x + 2)
    for s in range(4):
        for h in range(2):
            shalf(s, h).start()
    weight_grad(x + 1)
    weight_grad(x - 1)
    for s in range(4):
        for h in range(2):
            shalf(s, h).wait_recv()
            where = (slice(None), rows(o[s]), hcols(x + 1 - 2 * h, h))
            wg[where] = wg[where] + xh[s, h]
            sfull(s, h).start()
    weight_grad(x)

    returns = []
    for i in range(4):
        y2 = (y + STEPS[i]) % 4
        r = pl.ds(pl.multiple_of(y2 * 256, 256), 256)
        res = dot3((wsp[0, 0], wsp[1, 0]), (gd[0, 0, r, :], gd[1, 0, r, :]), NT)
        res = res + dot3((wsp[0, 1], wsp[1, 1]), (gd[0, 1, r, :], gd[1, 1, r, :]), NT)
        xs[y2 * 2, 0:448, :] = res[:, 0:128]
        xs[y2 * 2 + 1, 0:448, :] = res[:, 128:256]
        for n, (dc, dy) in enumerate(OTHERS):
            if dy == STEPS[i]:
                m = y2 * 2 + (c + dc) % 2
                cp = remote(
                    xs.at[m, pl.ds(0, 448), :], gx.at[me], ss_y.at[n], rs_y.at[n], dev(x, y2, z, c + dc)
                )
                cp.start()
                returns.append(cp)
    gx[me] = xs[me, 0:448, :]

    def total_x(s):
        sfull(s, 0).wait_recv()
        sfull(s, 1).wait_recv()
        where = (slice(None), rows(o[s]), cols(x))
        wg[where] = wg[where] + xf[s, 0] + xf[s, 1]

    def add(s, v):
        where = (slice(None), rows(o[s]), cols(x))
        wg[where] = wg[where] + v

    def add_half(s, h, v):
        where = (slice(None), rows(o[s]), hcols(x, h))
        wg[where] = wg[where] + v

    def zs(i, src, dst):
        return remote(src, dst, ss_s.at[i], rs_s.at[i], zp if i < 2 else zm)

    total_x(0)

    @pl.when(good)
    def _():
        zs(0, half(x, o[0], 0), zh.at[0]).start()
        zs(2, half(x, o[0], 1), zh.at[1]).start()

    @pl.when(bad)
    def _():
        zs(0, half(x, o[0], 0), zh.at[0]).wait_recv()
        add_half(0, 0, zh[0])
        zs(0, blk(x, o[0]), z1.at[0]).start()

    total_x(1)

    @pl.when(good)
    def _():
        zs(0, blk(x, o[1]), z1.at[0]).wait_recv()
        add(1, z1[0])
        zs(1, blk(x, o[1]), z2.at[0]).start()

    @pl.when(bad)
    def _():
        zs(2, half(x, o[1], 1), zh.at[1]).wait_recv()
        add_half(1, 1, zh[1])
        zs(2, blk(x, o[1]), z1.at[1]).start()

    total_x(2)

    @pl.when(good)
    def _():
        zs(2, blk(x, o[2]), z1.at[1]).wait_recv()
        add(2, z1[1])
        zs(3, blk(x, o[2]), z2.at[1]).start()

    @pl.when(bad)
    def _():
        zs(1, blk(x, o[2]), z2.at[0]).wait_recv()
        add(2, z2[0])
        zs(1, blk(x, o[2]), z3.at[0]).start()

    total_x(3)

    @pl.when(bad)
    def _():
        zs(3, blk(x, o[3]), z2.at[1]).wait_recv()
        add(3, z2[1])
        zs(3, blk(x, o[3]), z3.at[1]).start()

    for cp in returns:
        cp.wait()
    for j in range(28):
        t = jnp.concatenate([gx[m, to : to + n, :] for m, to, frm, n in PIECES[j]], axis=0)
        out[:, j * 128 : (j + 1) * 128] = t.T

    @pl.when(good)
    def _():
        zs(1, blk(x, o[3]), z3.at[0]).wait_recv()
        zs(3, blk(x, o[3]), z3.at[1]).wait_recv()
        add(3, z3[0] + z3[1])
        back = remote(half(x, o[3], 1 - yl), gout, ss_p.at[0], rs_p.at[3], partner)
        back.start()
        gout[...] = wg[:, rows(o[3]), hcols(x, yl)]
        back.wait_send()
        zs(0, half(x, o[0], 0), zh.at[0]).wait_send()
        zs(2, half(x, o[0], 1), zh.at[1]).wait_send()

    @pl.when(bad)
    def _():
        remote(half(x, o[3], 1 - yl), gout, ss_p.at[0], rs_p.at[3], partner).wait_recv()
        zs(0, blk(x, o[0]), z1.at[0]).wait_send()
        zs(2, blk(x, o[1]), z1.at[1]).wait_send()

    zs(1, blk(x, o[2]), z3.at[0]).wait_send()
    zs(3, blk(x, o[3]), z3.at[1]).wait_send()
    for s in range(4):
        for h in range(2):
            shalf(s, h).wait_send()
            sfull(s, h).wait_send()


def local(tokens, cotangent, routes, gates, w_gate, w_up, w_down):
    vm = pl.BlockSpec(memory_space=pltpu.VMEM)
    dma = pltpu.SemaphoreType.DMA
    full, hlf = (3, ROWS, 256), (3, ROWS, 128)

    def f32(*shape):
        return pltpu.VMEM(shape, F32)

    def bf16(*shape):
        return pltpu.VMEM(shape, BF16)

    out, gout = pl.pallas_call(
        kernel,
        out_shape=(jax.ShapeDtypeStruct((TOK, 3584), F32), jax.ShapeDtypeStruct(hlf, F32)),
        in_specs=[vm] * 7,
        out_specs=(vm, vm),
        scratch_shapes=[
            f32(8, 904, TOK), f32(8, 904, TOK), f32(3, 448, 1024), bf16(2, 3, 448, 1024),
            bf16(2, 2, 256, 448), bf16(2, 2, 448, 1024), f32(8, TOK, 8), f32(4, 2, TOK, 768),
            f32(4, TOK, 768), f32(3, TOK, 768), f32(4, 2, TOK, 768), bf16(2, 3, 1024, 1024),
            f32(8, 448, TOK), f32(4, 2, *hlf), f32(4, 2, *full),
            f32(2, *hlf), f32(2, *full), f32(2, *full), f32(2, *full),
            dma((4,)), dma((7,)), dma((7,)), dma((4,)), dma((4,)), dma((4,)), dma((4,)),
            dma((4, 4)), dma((4, 4)),
            dma((4,)), dma((4,)), dma((3,)), dma((3,)), dma((3,)), dma((3,)), dma((4,)), dma((4,)),
            dma((4, 2)), dma((4, 2)), dma((4, 2)), dma((4, 2)), dma((7,)), dma((7,)), dma((4,)), dma((4,)),
        ],
        compiler_params=pltpu.CompilerParams(
            collective_id=0, has_side_effects=True, vmem_limit_bytes=VMEM_LIMIT
        ),
        cost_estimate=pl.CostEstimate(flops=20_000_000_000, bytes_accessed=8_000_000, transcendentals=40_000),
    )(tokens, cotangent, routes, gates, w_gate[0], w_up[0], w_down[0])
    return out, gout[0:1], gout[1:2], gout[2:3]


def solution(mesh):
    rows = P(("dp", "expert"), None)
    weights = P("expert", "dp", None)
    return jax.shard_map(
        local,
        mesh=mesh,
        in_specs=(rows, rows, rows, rows, weights, weights, weights),
        out_specs=(rows, weights, weights, weights),
        check_vma=False,
    )
```

time: 478 us -> 193 us (0.40)
  waiting for transfers between devices: 344 us -> 0 us
  Pallas kernels: 0 us -> 184 us
  matrix products: 41.5 us -> 0 us
  local copies, waits for them, and re-layouts: 41.6 us -> 7.22 us
  other arithmetic: 20.2 us -> 0 us
  starting transfers between devices: 15 us -> 0 us
  between operations: 14 us -> 0.64 us
    pallas_call x0 -> x1, Pallas kernels: none -> 184 us  [local(): pl.pallas_call(kernel, out_shape=(jax.ShapeDtypeStruct((TOK, 3584), F32),...]
    all_gather x3 -> x0, waiting for transfers between devices: 171 us -> none  [the longest x1 104 us: local(): lax.all_gather(up_shard, 'dp', axis=0, tiled=True)]
    all_to_all x3 -> x0, waiting for transfers between devices: 129 us -> none  [the longest x1 65.2 us: local(): lax.all_to_all(row_grads.reshape(experts_here, capacity, model_width), 'e...]
    unnamed x5 -> x0, waiting for transfers between devices: 43.3 us -> none
    dot_general x7 -> x0, matrix products: 41.5 us -> none  [the longest x2 13.6 us: contract_rows(): lax.dot_general(left_side, right_side, (((0,), (0,)), ((), ())), precisio...]
    gather x4 -> x0, local copies, waits for them, and re-layouts: 22.9 us -> none  [the longest x1 8.79 us: local(): tokens[token_index]]
    all_to_all x3 -> x0, starting transfers between devices: 14.7 us -> none  [the longest x1 5.31 us: local(): lax.all_to_all(sent_rows, 'expert', split_axis=0, concat_axis=0, tiled=True)]
    select_n x3 -> x0, other arithmetic: 8.69 us -> none  [the longest x1 8.65 us: local(): jnp.where(filled, cotangent[token_index] * gates.reshape(-1)[source][:, N...]
  transfers between devices with their start and end apart: 7 -> 0, of which waited for: 5 -> 0; matrix products, arithmetic and copies ran while one was open for 16% -> 0% of each run, Pallas kernels for 0% -> 0%
where the time goes in v1:
time: 193 us; the launch traced here: 191 us
  Pallas kernels  184 us (95%)
  local copies, waits for them, and re-layouts  7.22 us (4%)
    pallas_call x1, Pallas kernels, local(): pl.pallas_call(kernel, out_shape=(jax.ShapeDtypeStruct((TOK, 3584), F32),...  184 us
    unnamed x3, local copies, waits for them, and re-layouts  5.67 us

profile of v1, /device:TPU:32, one launch (start us, length us, event | category | flops | bytes accessed | tf_op | source)
XLA Modules:
  0.0 191.5 jit_solution(2619442261663809344)
XLA Ops:
  0.6 1.4 copy.11.route
  2.0 1.4 copy.12.gate
  3.4 183.6 %shard_map.102 = (f32[128,3584]{1,0:T(8,128)}, f32[3,112,128]{2,1,0:T(8,128)}) custom-call(f32[128,3584]{1,0:T(8,128)} %tok.1, f32[128,3584]{1,0:T(8,128)} %cot.1, s32[128,2]{1,0:T(8,128)} %copy.11.route, f32[128,2]{1,0:T(8,128)} %copy.12.gate, f32[112,128]{1,0:T(8,128)} %bitcast.3, f32[112,128]{1,0:T(8,128)} %bitcast.4, f32[112,128]{1,0:T(8,128)} %bitcast.5), custom_call_target="tpu_custom_call" | custom-call | flops 20000000000 | bytes 8000000 | tf_op jit(solution)/shard_map/pallas_call | solution.py:535
  187.1 1.5 fusion
  188.6 2.9 %copy.14 = f32[128,3584]{1,0:T(8,128)} copy(f32[128,3584]{1,0:T(8,128)} %get-tuple-element.15) | data formatting | bytes 3670016

commit v2 on v1

--- a/solution.py
+++ b/solution.py
@@ -70,6 +70,7 @@
 def kernel(
     tok, cot, route, gate, w0, w1, w2, out, gout,
     xs, xg, wg, wsp, tsp, ttsp, infot, part, buf, got, ga, gd, gx, xh, xf, zh, z1, z2, z3,
+    y0, y1, y2b, y3, yh, yf, ss_bx, rs_bx, ss_bz, rs_bz, rs_by, rs_by2,
     s_l, ss_x, rs_x, ss_p, rs_p, ss_z, rs_z, ss_r, rs_r,
     ss_a, rs_a, ss_b, rs_b, ss_c, rs_c, ss_d, rs_d,
     ss_t, rs_t, ss_q, rs_q, ss_y, rs_y, ss_s, rs_s,
@@ -96,10 +97,19 @@
         return pl.ds(pl.multiple_of(((xx + 4) % 4) * 256 + h * 128, 128), 128)
 
     def blk(xx, b):
-        return wg.at[:, rows(b), cols(xx)]
+        return wg.at[0:2, rows(b), cols(xx)]
 
     def half(xx, b, h):
-        return wg.at[:, rows(b), hcols(xx, h)]
+        return wg.at[0:2, rows(b), hcols(xx, h)]
+
+    def chunk(b, q):
+        return wg.at[2, rows(b), pl.ds(q * 512, 512)]
+
+    def bblk(xx):
+        return wg.at[2, rows(zi), cols(xx)]
+
+    def bhalf(xx, h):
+        return wg.at[2, rows(zi), hcols(xx, h)]
 
     ws = (w0, w1, w2)
     local = [pltpu.make_async_copy(ws[k], wg.at[k, rows(zi), hcols(x, yl)], s_l.at[k]) for k in range(3)]
@@ -117,17 +127,7 @@
         for cp in shift:
             cp.start()
 
-    lane = lax.broadcasted_iota(jnp.int32, (TOK, TOK), 1)
-    facts = jnp.where(
-        lane == 0,
-        route[:, 0:1].astype(F32),
-        jnp.where(
-            lane == 1,
-            route[:, 1:2].astype(F32),
-            jnp.where(lane == 2, gate[:, 0:1], jnp.where(lane == 3, gate[:, 1:2], 0.0)),
-        ),
-    )
-    facts = facts.T[0:8]
+    facts = jnp.concatenate([route[...].astype(F32), gate[...], jnp.zeros((4, TOK), F32)], axis=0)
     for m in range(8):
         xs[m, 896:904, :] = facts
     for j in range(28):
@@ -173,6 +173,14 @@
         for i in range(4):
             (xcp(s, i, blk(x, b)) if i < 2 else xcp(s, i, half(x, b, 0))).wait_send()
 
+    def bx(i, ref):
+        return remote(ref, ref, ss_bx.at[i], rs_bx.at[i], xp if i % 2 == 0 else xm)
+
+    def bz(d, step, q, b):
+        return remote(
+            chunk(b, q), chunk(b, q), ss_bz.at[d, step, q], rs_bz.at[d, step, q], zm if d else zp
+        )
+
     @pl.when(good)
     def _():
         for k in range(3):
@@ -180,7 +188,18 @@
             remote(ws[k], wg.at[k, rows(zi), hcols(x, 1 - yl)], ss_p.at[k], rs_p.at[k], partner).wait_recv()
         zcp(0, blk(x, b0), zp).start()
         zcp(2, blk(x, b0), zm).start()
+        bx(0, bblk(x)).start()
+        bx(1, bblk(x)).start()
         start_x(0, b0)
+        bx(0, bblk(x - 1)).wait_recv()
+        bx(2, bhalf(x - 1, 0)).start()
+        bx(1, bblk(x + 1)).wait_recv()
+        bx(3, bhalf(x + 1, 1)).start()
+        bx(2, bhalf(x - 2, 0)).wait_recv()
+        bx(3, bhalf(x + 2, 1)).wait_recv()
+        for q in (0, 1):
+            bz(0, 0, q, b0).start()
+            bz(1, 0, 1 - q, b0).start()
 
     @pl.when(bad)
     def _():
@@ -202,6 +221,14 @@
         zcp(3, blk(x, b2), zm).start()
         start_x(2, b2)
 
+    @pl.when(bad)
+    def _():
+        for q in (0, 1):
+            bz(0, 0, q, b0).wait_recv()
+            bz(0, 0, q, b0).start()
+            bz(1, 0, 1 - q, b1).wait_recv()
+            bz(1, 0, 1 - q, b1).start()
+
     forward_x(1, b1)
 
     @pl.when(bad)
@@ -213,6 +240,14 @@
         zcp(3, half(x, b3, 1), zm).start()
         start_x(3, b3)
 
+    @pl.when(good)
+    def _():
+        for q in (0, 1):
+            bz(0, 0, q, b1).wait_recv()
+            bz(0, 1, q, b1).start()
+            bz(1, 0, 1 - q, b2).wait_recv()
+            bz(1, 1, 1 - q, b2).start()
+
     forward_x(2, b2)
 
     @pl.when(good)
@@ -220,17 +255,37 @@
         zcp(1, half(x, b3, 0), zp).wait_recv()
         zcp(3, half(x, b3, 1), zm).wait_recv()
         start_x(3, b3)
+
+    @pl.when(bad)
+    def _():
+        bz(0, 1, 0, b2).wait_recv()
+        bz(0, 1, 0, b2).start()
+        bz(1, 1, 1, b3).wait_recv()
+        bz(1, 1, 1, b3).start()
+        bz(0, 1, 1, b2).wait_recv()
+        bz(1, 1, 0, b3).wait_recv()
 
     forward_x(3, b3)
     for s, b in enumerate((b0, b1, b2, b3)):
         finish_x(s, b)
     zcp(0, blk(x, b0), zp).wait_send()
     zcp(2, blk(x, b0), zm).wait_send()
-
-    @pl.when(good)
-    def _():
+    for q in (0, 1):
+        bz(0, 0, q, b0).wait_send()
+        bz(1, 0, q, b0).wait_send()
+    bz(0, 1, 0, b0).wait_send()
+    bz(1, 1, 1, b0).wait_send()
+
+    @pl.when(good)
+    def _():
+        bz(0, 1, 0, b3).wait_recv()
+        bz(1, 1, 1, b3).wait_recv()
         zcp(1, blk(x, b1), zp).wait_send()
         zcp(3, blk(x, b1), zm).wait_send()
+        bz(0, 1, 1, b1).wait_send()
+        bz(1, 1, 0, b1).wait_send()
+        for i in range(4):
+            bx(i, bblk(x) if i < 2 else bhalf(x, 0)).wait_send()
 
     @pl.when(bad)
     def _():
@@ -320,7 +375,7 @@
         total = total + got[i]
 
     for k in range(2):
-        g = gate[:, k : k + 1]
+        g = infot[me, :, 2 + k : 3 + k]
         base = k * 384
         pre_gate = total[:, base : base + 128]
         pre_up = total[:, base + 128 : base + 256]
@@ -373,11 +428,14 @@
         cp.wait_send()
 
     def weight_grad(xx):
-        for kind in range(3):
-            a = 1 if kind == 2 else 0
+        for kind in range(2):
             wg[kind, :, cols(xx)] = dot3(
-                (ttsp[0, a], ttsp[1, a]), (gd[0, kind, :, cols(xx)], gd[1, kind, :, cols(xx)]), NN
+                (ttsp[0, 0], ttsp[1, 0]), (gd[0, kind, :, cols(xx)], gd[1, kind, :, cols(xx)]), NN
             )
+
+    def weight_grad_b(q):
+        cs = slice(q * 512, q * 512 + 512)
+        wg[2, :, cs] = dot3((ttsp[0, 1], ttsp[1, 1]), (gd[0, 2, :, cs], gd[1, 2, :, cs]), NN)
 
     o = [jnp.where(good, p, q) for p, q in ((zi + 2, hi + 1), (zi + 1, lo - 1), (zi - 1, hi), (zi, lo))]
 
@@ -391,22 +449,77 @@
             blk(x + 1 - 2 * h, o[s]), xf.at[s, h], ss_q.at[s, h], rs_q.at[s, h], xp if h == 0 else xm
         )
 
+    def by(d, step, q, b, dst):
+        return remote(
+            chunk(b, q), dst.at[d, :, pl.ds(q * 512, 512)],
+            ss_bz.at[d, step, q], rs_by.at[d, step, q], zm if d else zp,
+        )
+
+    def take(d, step, q, b, dst):
+        by(d, step, q, b, dst).wait_recv()
+        where = (2, rows(b), slice(q * 512, q * 512 + 512))
+        wg[where] = wg[where] + dst[d, :, q * 512 : q * 512 + 512]
+
     weight_grad(x + 2)
     for s in range(4):
         for h in range(2):
             shalf(s, h).start()
+    weight_grad_b(0)
+
+    @pl.when(good)
+    def _():
+        by(0, 0, 0, zi + 2, y0).start()
+
+    @pl.when(bad)
+    def _():
+        by(1, 0, 0, lo - 1, y1).start()
+
+    weight_grad_b(1)
+
+    @pl.when(good)
+    def _():
+        by(1, 0, 1, zi + 2, y0).start()
+
+    @pl.when(bad)
+    def _():
+        by(0, 0, 1, hi + 1, y1).start()
+
     weight_grad(x + 1)
     weight_grad(x - 1)
+
+    @pl.when(bad)
+    def _():
+        take(0, 0, 0, hi + 1, y0)
+        by(0, 0, 0, hi + 1, y1).start()
+        take(1, 0, 1, lo - 1, y0)
+        by(1, 0, 1, lo - 1, y1).start()
+
     for s in range(4):
         for h in range(2):
             shalf(s, h).wait_recv()
-            where = (slice(None), rows(o[s]), hcols(x + 1 - 2 * h, h))
+            where = (slice(0, 2), rows(o[s]), hcols(x + 1 - 2 * h, h))
             wg[where] = wg[where] + xh[s, h]
             sfull(s, h).start()
+
+    @pl.when(good)
+    def _():
+        take(0, 0, 1, zi + 1, y1)
+        by(0, 1, 1, zi + 1, y2b).start()
+        take(1, 0, 0, zi - 1, y1)
+        by(1, 1, 0, zi - 1, y2b).start()
+
     weight_grad(x)
 
+    @pl.when(good)
+    def _():
+        take(0, 0, 0, zi + 1, y1)
+        by(0, 1, 0, zi + 1, y2b).start()
+        take(1, 0, 1, zi - 1, y1)
+        by(1, 1, 1, zi - 1, y2b).start()
+
     returns = []
-    for i in range(4):
+
+    def token_grad(i):
         y2 = (y + STEPS[i]) % 4
         r = pl.ds(pl.multiple_of(y2 * 256, 256), 256)
         res = dot3((wsp[0, 0], wsp[1, 0]), (gd[0, 0, r, :], gd[1, 0, r, :]), NT)
@@ -421,20 +534,41 @@
                 )
                 cp.start()
                 returns.append(cp)
+
+    token_grad(0)
+    token_grad(1)
+
+    @pl.when(bad)
+    def _():
+        take(0, 1, 1, hi, y2b)
+        by(0, 1, 1, hi, y3).start()
+        take(1, 1, 0, lo, y2b)
+        by(1, 1, 0, lo, y3).start()
+
+    token_grad(2)
+
+    @pl.when(bad)
+    def _():
+        take(0, 1, 0, hi, y2b)
+        by(0, 1, 0, hi, y3).start()
+        take(1, 1, 1, lo, y2b)
+        by(1, 1, 1, lo, y3).start()
+
+    token_grad(3)
     gx[me] = xs[me, 0:448, :]
 
     def total_x(s):
         sfull(s, 0).wait_recv()
         sfull(s, 1).wait_recv()
-        where = (slice(None), rows(o[s]), cols(x))
+        where = (slice(0, 2), rows(o[s]), cols(x))
         wg[where] = wg[where] + xf[s, 0] + xf[s, 1]
 
     def add(s, v):
-        where = (slice(None), rows(o[s]), cols(x))
+        where = (slice(0, 2), rows(o[s]), cols(x))
         wg[where] = wg[where] + v
 
     def add_half(s, h, v):
-        where = (slice(None), rows(o[s]), hcols(x, h))
+        where = (slice(0, 2), rows(o[s]), hcols(x, h))
         wg[where] = wg[where] + v
 
     def zs(i, src, dst):
@@ -467,10 +601,29 @@
         add_half(1, 1, zh[1])
         zs(2, blk(x, o[1]), z1.at[1]).start()
 
+    def bh(h):
+        return remote(bhalf(x + 2, h), yh.at[h], ss_bx.at[h], rs_by2.at[h], xm if h else xp)
+
+    def bf(h):
+        return remote(bblk(x + 1 - 2 * h), yf.at[h], ss_bx.at[2 + h], rs_by2.at[2 + h], xm if h else xp)
+
+    @pl.when(good)
+    def _():
+        for q in (0, 1):
+            take(0, 1, 1 - q, zi, y3)
+            take(1, 1, q, zi, y3)
+        bh(0).start()
+        bh(1).start()
+
     total_x(2)
 
     @pl.when(good)
     def _():
+        for h in range(2):
+            bh(h).wait_recv()
+            where = (2, rows(zi), hcols(x + 1 - 2 * h, h))
+            wg[where] = wg[where] + yh[h]
+            bf(h).start()
         zs(2, blk(x, o[2]), z1.at[1]).wait_recv()
         add(2, z1[1])
         zs(3, blk(x, o[2]), z2.at[1]).start()
@@ -500,19 +653,34 @@
         zs(1, blk(x, o[3]), z3.at[0]).wait_recv()
         zs(3, blk(x, o[3]), z3.at[1]).wait_recv()
         add(3, z3[0] + z3[1])
-        back = remote(half(x, o[3], 1 - yl), gout, ss_p.at[0], rs_p.at[3], partner)
+        bf(0).wait_recv()
+        bf(1).wait_recv()
+        where = (2, rows(zi), cols(x))
+        wg[where] = wg[where] + yf[0] + yf[1]
+        back = remote(wg.at[:, rows(zi), hcols(x, 1 - yl)], gout, ss_p.at[0], rs_p.at[3], partner)
         back.start()
-        gout[...] = wg[:, rows(o[3]), hcols(x, yl)]
+        gout[...] = wg[:, rows(zi), hcols(x, yl)]
         back.wait_send()
         zs(0, half(x, o[0], 0), zh.at[0]).wait_send()
         zs(2, half(x, o[0], 1), zh.at[1]).wait_send()
-
-    @pl.when(bad)
-    def _():
-        remote(half(x, o[3], 1 - yl), gout, ss_p.at[0], rs_p.at[3], partner).wait_recv()
+        by(0, 0, 0, zi + 2, y0).wait_send()
+        by(1, 0, 1, zi + 2, y0).wait_send()
+        for h in range(2):
+            bh(h).wait_send()
+            bf(h).wait_send()
+
+    @pl.when(bad)
+    def _():
+        remote(wg.at[:, rows(zi), hcols(x, 1 - yl)], gout, ss_p.at[0], rs_p.at[3], partner).wait_recv()
         zs(0, blk(x, o[0]), z1.at[0]).wait_send()
         zs(2, blk(x, o[1]), z1.at[1]).wait_send()
-
+        for q in (0, 1):
+            by(0, 0, q, hi + 1, y1).wait_send()
+            by(1, 0, q, lo - 1, y1).wait_send()
+
+    for q in (0, 1):
+        by(0, 1, q, zi, y2b).wait_send()
+        by(1, 1, q, zi, y2b).wait_send()
     zs(1, blk(x, o[2]), z3.at[0]).wait_send()
     zs(3, blk(x, o[3]), z3.at[1]).wait_send()
     for s in range(4):
@@ -524,7 +692,7 @@
 def local(tokens, cotangent, routes, gates, w_gate, w_up, w_down):
     vm = pl.BlockSpec(memory_space=pltpu.VMEM)
     dma = pltpu.SemaphoreType.DMA
-    full, hlf = (3, ROWS, 256), (3, ROWS, 128)
+    full, hlf = (2, ROWS, 256), (2, ROWS, 128)
 
     def f32(*shape):
         return pltpu.VMEM(shape, F32)
@@ -534,7 +702,7 @@
 
     out, gout = pl.pallas_call(
         kernel,
-        out_shape=(jax.ShapeDtypeStruct((TOK, 3584), F32), jax.ShapeDtypeStruct(hlf, F32)),
+        out_shape=(jax.ShapeDtypeStruct((TOK, 3584), F32), jax.ShapeDtypeStruct((3, ROWS, 128), F32)),
         in_specs=[vm] * 7,
         out_specs=(vm, vm),
         scratch_shapes=[
@@ -543,6 +711,9 @@
             f32(4, TOK, 768), f32(3, TOK, 768), f32(4, 2, TOK, 768), bf16(2, 3, 1024, 1024),
             f32(8, 448, TOK), f32(4, 2, *hlf), f32(4, 2, *full),
             f32(2, *hlf), f32(2, *full), f32(2, *full), f32(2, *full),
+            f32(2, ROWS, 1024), f32(2, ROWS, 1024), f32(2, ROWS, 1024), f32(2, ROWS, 1024),
+            f32(2, ROWS, 128), f32(2, ROWS, 256),
+            dma((4,)), dma((4,)), dma((2, 2, 2)), dma((2, 2, 2)), dma((2, 2, 2)), dma((4,)),
             dma((4,)), dma((7,)), dma((7,)), dma((4,)), dma((4,)), dma((4,)), dma((4,)),
             dma((4, 4)), dma((4, 4)),
             dma((4,)), dma((4,)), dma((3,)), dma((3,)), dma((3,)), dma((3,)), dma((4,)), dma((4,)),
@@ -552,7 +723,7 @@
             collective_id=0, has_side_effects=True, vmem_limit_bytes=VMEM_LIMIT
         ),
         cost_estimate=pl.CostEstimate(flops=20_000_000_000, bytes_accessed=8_000_000, transcendentals=40_000),
-    )(tokens, cotangent, routes, gates, w_gate[0], w_up[0], w_down[0])
+    )(tokens, cotangent, routes.T, gates.T, w_gate[0], w_up[0], w_down[0])
     return out, gout[0:1], gout[1:2], gout[2:3]
 
 

time: 193 us -> 175 us (0.907); the launches traced: 191 us -> 171 us
  Pallas kernels: 184 us -> 166 us
  local copies, waits for them, and re-layouts: 7.22 us -> 4.4 us
    pallas_call x1, Pallas kernels: 184 us -> 166 us  [local(): pl.pallas_call(kernel, out_shape=(jax.ShapeDtypeStruct((TOK, 3584), F32),...]
    unnamed x3 -> x1, local copies, waits for them, and re-layouts: 5.67 us -> 2.86 us
where the time goes in v2:
time: 175 us; the launch traced here: 171 us
  Pallas kernels  166 us (95%)
  local copies, waits for them, and re-layouts  4.4 us (3%)
    pallas_call x1, Pallas kernels, local(): pl.pallas_call(kernel, out_shape=(jax.ShapeDtypeStruct((TOK, 3584), F32),...  166 us

profile of v2, /device:TPU:32, one launch (start us, length us, event | category | flops | bytes accessed | tf_op | source)
XLA Modules:
  0.0 171.1 jit_solution(4673540027451451662)
XLA Ops:
  0.6 166.1 %shard_map.102 = (f32[128,3584]{1,0:T(8,128)}, f32[3,112,128]{2,1,0:T(8,128)}) custom-call(f32[128,3584]{1,0:T(8,128)} %tok.1, f32[128,3584]{1,0:T(8,128)} %cot.1, s32[2,128]{1,0:T(2,128)} %bitcast.8, f32[2,128]{1,0:T(2,128)} %bitcast.9, f32[112,128]{1,0:T(8,128)} %bitcast.5, f32[112,128]{1,0:T(8,128)} %bitcast.6, f32[112,128]{1,0:T(8,128)} %bitcast.7), custom_call_target="tpu_custom_call" | custom-call | flops 20000000000 | bytes 8000000 | tf_op jit(solution)/shard_map/pallas_call | solution.py:703
  166.7 1.5 fusion
  168.2 2.9 %copy.12 = f32[128,3584]{1,0:T(8,128)} copy(f32[128,3584]{1,0:T(8,128)} %get-tuple-element.15) | data formatting | bytes 3670016

commit v3 on v2

--- a/solution.py
+++ b/solution.py
@@ -69,9 +69,9 @@
 
 def kernel(
     tok, cot, route, gate, w0, w1, w2, out, gout,
-    xs, xg, wg, wsp, tsp, ttsp, infot, part, buf, got, ga, gd, gx, xh, xf, zh, z1, z2, z3,
+    xs, xc, xg, cg, wg, wsp, tsp, csp, ttsp, infot, part, buf, got_h, got, ga, gd, xh, xf, zh, z1, z2, z3,
     y0, y1, y2b, y3, yh, yf, ss_bx, rs_bx, ss_bz, rs_bz, rs_by, rs_by2,
-    s_l, ss_x, rs_x, ss_p, rs_p, ss_z, rs_z, ss_r, rs_r,
+    s_l, ss_x, rs_x, ss_xc, rs_xc, ss_p, rs_p, ss_z, rs_z, ss_r, rs_r,
     ss_a, rs_a, ss_b, rs_b, ss_c, rs_c, ss_d, rs_d,
     ss_t, rs_t, ss_q, rs_q, ss_y, rs_y, ss_s, rs_s,
 ):
@@ -129,20 +129,50 @@
 
     facts = jnp.concatenate([route[...].astype(F32), gate[...], jnp.zeros((4, TOK), F32)], axis=0)
     for m in range(8):
-        xs[m, 896:904, :] = facts
-    for j in range(28):
-        for a, ref in ((0, tok), (1, cot)):
+        xs[m, 448:456, :] = facts
+
+    def transpose(ref, dst):
+        for j in range(28):
             t = ref[:, j * 128 : (j + 1) * 128].T
             for m, to, frm, n in PIECES[j]:
-                xs[m, a * 448 + to : a * 448 + to + n, :] = t[frm : frm + n]
+                dst[m, to : to + n, :] = t[frm : frm + n]
+
+    def group(src, dst, ss, rs):
+        cps = []
+        for i, (dc, dy) in enumerate(OTHERS):
+            y2, c2 = (y + dy) % 4, (c + dc) % 2
+            cps.append(remote(src.at[y2 * 2 + c2], dst.at[me], ss.at[i], rs.at[i], dev(x, y2, z, c2)))
+        return cps
+
+    transpose(tok, xs)
     keep = pltpu.make_async_copy(xs.at[me], xg.at[me], s_l.at[3])
     keep.start()
-    tokens_out = []
-    for i, (dc, dy) in enumerate(OTHERS):
-        y2, c2 = (y + dy) % 4, (c + dc) % 2
-        cp = remote(xs.at[y2 * 2 + c2], xg.at[me], ss_x.at[i], rs_x.at[i], dev(x, y2, z, c2))
+    tokens_out = group(xs, xg, ss_x, rs_x)
+    for cp in tokens_out:
         cp.start()
-        tokens_out.append(cp)
+    transpose(cot, xc)
+    keep_c = pltpu.make_async_copy(xc.at[me], cg.at[me], s_l.at[4])
+    keep_c.start()
+    cot_out = group(xc, cg, ss_xc, rs_xc)
+
+    def member_rows(y2, c2):
+        return pl.ds(pl.multiple_of(y2 * 256 + c2 * 128, 128), 128)
+
+    def prepare_t(y2):
+        for c2 in range(2):
+            m = y2 * 2 + c2
+            infot[m, :, 0:8] = xg[m, 448:456, :].T
+            v = xg[m, 0:448, :]
+            r = member_rows(y2, c2)
+            ttsp[0, 0, :, r], ttsp[1, 0, :, r] = split(v)
+            tsp[0, r, :], tsp[1, r, :] = split(v.T)
+
+    def prepare_c(y2):
+        for c2 in range(2):
+            v = cg[y2 * 2 + c2]
+            r = member_rows(y2, c2)
+            ttsp[0, 1, :, r], ttsp[1, 1, :, r] = split(v)
+            csp[0, c2 * 128 : (c2 + 1) * 128, :], csp[1, c2 * 128 : (c2 + 1) * 128, :] = split(v.T)
 
     lo = (z - 1 - yl + 8) // 2
     hi = lo + 1
@@ -248,6 +278,10 @@
             bz(1, 0, 1 - q, b2).wait_recv()
             bz(1, 1, 1 - q, b2).start()
 
+    for cp in tokens_out:
+        cp.wait_send()
+    for cp in cot_out:
+        cp.start()
     forward_x(2, b2)
 
     @pl.when(good)
@@ -265,6 +299,11 @@
         bz(0, 1, 1, b2).wait_recv()
         bz(1, 1, 0, b3).wait_recv()
 
+    keep.wait()
+    for cp in tokens_out:
+        cp.wait_recv()
+    for i in range(4):
+        prepare_t((y + i) % 4)
     forward_x(3, b3)
     for s, b in enumerate((b0, b1, b2, b3)):
         finish_x(s, b)
@@ -294,40 +333,25 @@
         for cp in shift:
             cp.wait_send()
 
-    def split_w(i, _):
-        r = pl.ds(pl.multiple_of(i * 32, 32), 32)
-        for k in range(3):
-            h, l = split(wg[k, r, :])
-            wsp[0, k, r, :] = h
-            wsp[1, k, r, :] = l
-        return 0
-
-    lax.fori_loop(0, 14, split_w, 0)
-
-    def member_rows(y2, c2):
-        return pl.ds(pl.multiple_of(y2 * 256 + c2 * 128, 128), 128)
-
-    def prepare(y2):
-        for c2 in range(2):
-            m = y2 * 2 + c2
-            infot[m, :, 0:8] = xg[m, 896:904, :].T
-            for a in range(2):
-                v = xg[m, a * 448 : (a + 1) * 448, :]
-                h, l = split(v)
-                ttsp[0, a, :, member_rows(y2, c2)] = h
-                ttsp[1, a, :, member_rows(y2, c2)] = l
-                h, l = split(v.T)
-                tsp[0, a, c2 * 128 : (c2 + 1) * 128, :] = h
-                tsp[1, a, c2 * 128 : (c2 + 1) * 128, :] = l
-
-    def forward(y2):
+    def split_w(kinds):
+        def step(i, _):
+            r = pl.ds(pl.multiple_of(i * 32, 32), 32)
+            for k in kinds:
+                h, l = split(wg[k, r, :])
+                wsp[0, k, r, :] = h
+                wsp[1, k, r, :] = l
+            return 0
+
+        lax.fori_loop(0, 14, step, 0)
+
+    def forward(y2, kinds):
         r = [
             jnp.concatenate([infot[y2 * 2, :, k : k + 1], infot[y2 * 2 + 1, :, k : k + 1]], axis=0)
             for k in range(2)
         ]
-        for kind in range(3):
-            a = 1 if kind == 2 else 0
-            t = tsp[0, a], tsp[1, a]
+        rr = pl.ds(pl.multiple_of(y2 * 256, 256), 256)
+        for kind in kinds:
+            t = (csp[0], csp[1]) if kind == 2 else (tsp[0, rr, :], tsp[1, rr, :])
             sel = [jnp.zeros((256, 128), F32)] * 2
             for q in range(4):
                 cs = slice(q * 256, (q + 1) * 256)
@@ -336,50 +360,81 @@
                     for k in range(2):
                         sel[k] = jnp.where(r[k] == float(q * 2 + e), res[:, e * 128 : (e + 1) * 128], sel[k])
             for k in range(2):
-                base = (k * 3 + kind) * 128
+                base = (kind * 2 + k) * 128
                 part[y2, 0, :, base : base + 128] = sel[k][0:128]
                 part[y2, 1, :, base : base + 128] = sel[k][128:256]
 
     STEPS = (2, 1, 3, 0)
-
-    def first(i):
+    COLS = (pl.ds(0, 512), pl.ds(512, 256))
+
+    def first(p, i):
         y2 = (y + STEPS[i]) % 4
-        return remote(part.at[y2, 1 - c], buf.at[y2], ss_a.at[i], rs_a.at[i], sib)
-
-    def second(i):
+        return remote(
+            part.at[y2, 1 - c, :, COLS[p]], buf.at[y2, :, COLS[p]], ss_a.at[p, i], rs_a.at[p, i], sib
+        )
+
+    yp, ym = dev(x, y + 1, z, c), dev(x, y - 1, z, c)
+
+    def ring_half(p, h):
+        return remote(
+            buf.at[(y + 2) % 4, pl.ds(64 * h, 64), COLS[p]], got_h.at[h, :, COLS[p]],
+            ss_b.at[p, h], rs_b.at[p, h], ym if h else yp,
+        )
+
+    def ring_full(p, h):
+        return remote(
+            buf.at[(y + 1 + 2 * h) % 4, :, COLS[p]], got.at[h, :, COLS[p]],
+            ss_b.at[p, 2 + h], rs_b.at[p, 2 + h], ym if h else yp,
+        )
+
+    def merge(p, i):
         y2 = (y + STEPS[i]) % 4
-        return remote(buf.at[y2], got.at[i], ss_b.at[i], rs_b.at[i], dev(x, y2, z, c))
-
-    def merge(i):
-        y2 = (y + STEPS[i]) % 4
-        first(i).wait_recv()
-        buf[y2] = buf[y2] + part[y2, c]
-        if i < 3:
-            second(i).start()
-
-    keep.wait()
+        first(p, i).wait_recv()
+        buf[y2, :, COLS[p]] = buf[y2, :, COLS[p]] + part[y2, c, :, COLS[p]]
+        if i == 0:
+            ring_half(p, 0).start()
+            ring_half(p, 1).start()
+        elif i < 3:
+            h = i - 1
+            ring_half(p, h).wait_recv()
+            r = pl.ds(64 * h, 64)
+            buf[y2, r, COLS[p]] = buf[y2, r, COLS[p]] + got_h[h, :, COLS[p]]
+            ring_full(p, h).start()
+
+    split_w((0, 1))
+    for i in range(4):
+        forward((y + STEPS[i]) % 4, (0, 1))
+        first(0, i).start()
+        if i == 1:
+            merge(0, 0)
+    split_w((2,))
+    merge(0, 1)
+    keep_c.wait()
     for i in range(4):
         y2 = (y + STEPS[i]) % 4
         for n, (dc, dy) in enumerate(OTHERS):
             if (4 - dy) % 4 == STEPS[i]:
-                tokens_out[n].wait_recv()
-        prepare(y2)
-        forward(y2)
-        first(i).start()
-        if i:
-            merge(i - 1)
-    merge(3)
-    total = buf[y]
-    for i in range(3):
-        second(i).wait_recv()
-        total = total + got[i]
+                cot_out[n].wait_recv()
+        prepare_c(y2)
+        forward(y2, (2,))
+        first(1, i).start()
+        if i == 0:
+            merge(0, 2)
+            merge(0, 3)
+        else:
+            merge(1, i - 1)
+    merge(1, 3)
+    for p in range(2):
+        for h in range(2):
+            ring_full(p, h).wait_recv()
+    total = buf[y] + got[0] + got[1]
 
     for k in range(2):
         g = infot[me, :, 2 + k : 3 + k]
         base = k * 384
-        pre_gate = total[:, base : base + 128]
-        pre_up = total[:, base + 128 : base + 256]
-        back = total[:, base + 256 : base + 384] * g
+        pre_gate = total[:, k * 128 : k * 128 + 128]
+        pre_up = total[:, k * 128 + 256 : k * 128 + 384]
+        back = total[:, k * 128 + 512 : k * 128 + 640] * g
         s = jax.nn.sigmoid(pre_gate)
         activated = pre_gate * s
         slopes = s * (1.0 + pre_gate * (1.0 - s))
@@ -387,8 +442,12 @@
         ga[y, c, :, base + 128 : base + 256] = back * activated
         ga[y, c, :, base + 256 : base + 384] = activated * pre_up * g
 
-    def spread(i):
-        return remote(ga.at[y, c], ga.at[y, c], ss_c.at[i], rs_c.at[i], dev(x, y + STEPS[i], z, c))
+    def spread(h):
+        return remote(ga.at[y, c], ga.at[y, c], ss_c.at[h], rs_c.at[h], ym if h else yp)
+
+    def spread_half(h, y2):
+        ref = ga.at[y2 % 4, c, pl.ds(64 * h, 64), :]
+        return remote(ref, ref, ss_c.at[2 + h], rs_c.at[2 + h], ym if h else yp)
 
     def pass_on(i, y2):
         return remote(ga.at[y2, c], ga.at[y2, c], ss_d.at[i], rs_d.at[i], sib)
@@ -405,26 +464,43 @@
                 gd[0, kind, member_rows(y2, c2), e * 128 : (e + 1) * 128] = h
                 gd[1, kind, member_rows(y2, c2), e * 128 : (e + 1) * 128] = l
 
-    for i in range(3):
-        spread(i).start()
+    spread(0).start()
+    spread(1).start()
     pass_on(3, y).start()
     expand(y, c)
-    for i in (1, 2, 0):
-        y2 = (y - STEPS[i] + 4) % 4
-        remote(ga.at[y2, c], ga.at[y2, c], ss_c.at[i], rs_c.at[i], dev(x, y2, z, c)).wait_recv()
-        pass_on(i, y2).start()
-        expand(y2, c)
-    for i in (3, 1, 2, 0):
-        y2 = (y - STEPS[i] + 4) % 4
-        remote(ga.at[y2, 1 - c], ga.at[y2, 1 - c], ss_d.at[i], rs_d.at[i], sib).wait_recv()
+    for h in range(2):
+        y2 = (y + 3 + 2 * h) % 4
+        ref = ga.at[y2, c]
+        remote(ref, ref, ss_c.at[h], rs_c.at[h], ym if h else yp).wait_recv()
+        spread_half(h, y2).start()
+        pass_on(h, y2).start()
+    arrived = remote(ga.at[y, 1 - c], ga.at[y, 1 - c], ss_d.at[3], rs_d.at[3], sib)
+    arrived.wait_recv()
+    expand(y, 1 - c)
+    for h in range(2):
+        expand((y + 3 + 2 * h) % 4, c)
+    far = (y + 2) % 4
+    spread_half(0, y + 2).wait_recv()
+    spread_half(1, y + 2).wait_recv()
+    pass_on(2, far).start()
+    for h in range(2):
+        y2 = (y + 3 + 2 * h) % 4
+        remote(ga.at[y2, 1 - c], ga.at[y2, 1 - c], ss_d.at[h], rs_d.at[h], sib).wait_recv()
         expand(y2, 1 - c)
+    expand(far, c)
+    remote(ga.at[far, 1 - c], ga.at[far, 1 - c], ss_d.at[2], rs_d.at[2], sib).wait_recv()
+    expand(far, 1 - c)
     for i in range(4):
-        first(i).wait_send()
+        first(0, i).wait_send()
+        first(1, i).wait_send()
         pass_on(i, y).wait_send()
-    for i in range(3):
-        second(i).wait_send()
-        spread(i).wait_send()
-    for cp in tokens_out:
+    for h in range(2):
+        for p in range(2):
+            ring_half(p, h).wait_send()
+            ring_full(p, h).wait_send()
+        spread(h).wait_send()
+        spread_half(h, y).wait_send()
+    for cp in cot_out:
         cp.wait_send()
 
     def weight_grad(xx):
@@ -530,32 +606,10 @@
             if dy == STEPS[i]:
                 m = y2 * 2 + (c + dc) % 2
                 cp = remote(
-                    xs.at[m, pl.ds(0, 448), :], gx.at[me], ss_y.at[n], rs_y.at[n], dev(x, y2, z, c + dc)
+                    xs.at[m, pl.ds(0, 448), :], cg.at[me], ss_y.at[n], rs_y.at[n], dev(x, y2, z, c + dc)
                 )
                 cp.start()
                 returns.append(cp)
-
-    token_grad(0)
-    token_grad(1)
-
-    @pl.when(bad)
-    def _():
-        take(0, 1, 1, hi, y2b)
-        by(0, 1, 1, hi, y3).start()
-        take(1, 1, 0, lo, y2b)
-        by(1, 1, 0, lo, y3).start()
-
-    token_grad(2)
-
-    @pl.when(bad)
-    def _():
-        take(0, 1, 0, hi, y2b)
-        by(0, 1, 0, hi, y3).start()
-        take(1, 1, 1, lo, y2b)
-        by(1, 1, 1, lo, y3).start()
-
-    token_grad(3)
-    gx[me] = xs[me, 0:448, :]
 
     def total_x(s):
         sfull(s, 0).wait_recv()
@@ -574,12 +628,28 @@
     def zs(i, src, dst):
         return remote(src, dst, ss_s.at[i], rs_s.at[i], zp if i < 2 else zm)
 
+    def bh(h):
+        return remote(bhalf(x + 2, h), yh.at[h], ss_bx.at[h], rs_by2.at[h], xm if h else xp)
+
+    def bf(h):
+        return remote(bblk(x + 1 - 2 * h), yf.at[h], ss_bx.at[2 + h], rs_by2.at[2 + h], xm if h else xp)
+
+    token_grad(0)
     total_x(0)
 
     @pl.when(good)
     def _():
         zs(0, half(x, o[0], 0), zh.at[0]).start()
         zs(2, half(x, o[0], 1), zh.at[1]).start()
+
+    @pl.when(bad)
+    def _():
+        take(0, 1, 1, hi, y2b)
+        by(0, 1, 1, hi, y3).start()
+        take(1, 1, 0, lo, y2b)
+        by(1, 1, 0, lo, y3).start()
+
+    token_grad(1)
 
     @pl.when(bad)
     def _():
@@ -589,33 +659,51 @@
 
     total_x(1)
 
+    @pl.when(bad)
+    def _():
+        zs(2, half(x, o[1], 1), zh.at[1]).wait_recv()
+        add_half(1, 1, zh[1])
+        zs(2, blk(x, o[1]), z1.at[1]).start()
+        take(0, 1, 0, hi, y2b)
+        by(0, 1, 0, hi, y3).start()
+        take(1, 1, 1, lo, y2b)
+        by(1, 1, 1, lo, y3).start()
+
+    token_grad(2)
+    token_grad(3)
+
     @pl.when(good)
     def _():
         zs(0, blk(x, o[1]), z1.at[0]).wait_recv()
         add(1, z1[0])
         zs(1, blk(x, o[1]), z2.at[0]).start()
 
-    @pl.when(bad)
-    def _():
-        zs(2, half(x, o[1], 1), zh.at[1]).wait_recv()
-        add_half(1, 1, zh[1])
-        zs(2, blk(x, o[1]), z1.at[1]).start()
-
-    def bh(h):
-        return remote(bhalf(x + 2, h), yh.at[h], ss_bx.at[h], rs_by2.at[h], xm if h else xp)
-
-    def bf(h):
-        return remote(bblk(x + 1 - 2 * h), yf.at[h], ss_bx.at[2 + h], rs_by2.at[2 + h], xm if h else xp)
-
-    @pl.when(good)
-    def _():
+    total_x(2)
+
+    @pl.when(good)
+    def _():
+        zs(2, blk(x, o[2]), z1.at[1]).wait_recv()
+        add(2, z1[1])
+        zs(3, blk(x, o[2]), z2.at[1]).start()
         for q in (0, 1):
             take(0, 1, 1 - q, zi, y3)
             take(1, 1, q, zi, y3)
         bh(0).start()
         bh(1).start()
 
-    total_x(2)
+    @pl.when(bad)
+    def _():
+        zs(1, blk(x, o[2]), z2.at[0]).wait_recv()
+        add(2, z2[0])
+        zs(1, blk(x, o[2]), z3.at[0]).start()
+
+    total_x(3)
+
+    @pl.when(bad)
+    def _():
+        zs(3, blk(x, o[3]), z2.at[1]).wait_recv()
+        add(3, z2[1])
+        zs(3, blk(x, o[3]), z3.at[1]).start()
 
     @pl.when(good)
     def _():
@@ -624,43 +712,31 @@
             where = (2, rows(zi), hcols(x + 1 - 2 * h, h))
             wg[where] = wg[where] + yh[h]
             bf(h).start()
-        zs(2, blk(x, o[2]), z1.at[1]).wait_recv()
-        add(2, z1[1])
-        zs(3, blk(x, o[2]), z2.at[1]).start()
-
-    @pl.when(bad)
-    def _():
-        zs(1, blk(x, o[2]), z2.at[0]).wait_recv()
-        add(2, z2[0])
-        zs(1, blk(x, o[2]), z3.at[0]).start()
-
-    total_x(3)
-
-    @pl.when(bad)
-    def _():
-        zs(3, blk(x, o[3]), z2.at[1]).wait_recv()
-        add(3, z2[1])
-        zs(3, blk(x, o[3]), z3.at[1]).start()
+
+    cg[me] = xs[me, 0:448, :]
 
     for cp in returns:
         cp.wait()
     for j in range(28):
-        t = jnp.concatenate([gx[m, to : to + n, :] for m, to, frm, n in PIECES[j]], axis=0)
+        t = jnp.concatenate([cg[m, to : to + n, :] for m, to, frm, n in PIECES[j]], axis=0)
         out[:, j * 128 : (j + 1) * 128] = t.T
 
     @pl.when(good)
     def _():
-        zs(1, blk(x, o[3]), z3.at[0]).wait_recv()
-        zs(3, blk(x, o[3]), z3.at[1]).wait_recv()
-        add(3, z3[0] + z3[1])
         bf(0).wait_recv()
         bf(1).wait_recv()
         where = (2, rows(zi), cols(x))
         wg[where] = wg[where] + yf[0] + yf[1]
-        back = remote(wg.at[:, rows(zi), hcols(x, 1 - yl)], gout, ss_p.at[0], rs_p.at[3], partner)
+        back_b = remote(bhalf(x, 1 - yl), gout.at[2], ss_p.at[1], rs_p.at[4], partner)
+        back_b.start()
+        zs(1, blk(x, o[3]), z3.at[0]).wait_recv()
+        zs(3, blk(x, o[3]), z3.at[1]).wait_recv()
+        add(3, z3[0] + z3[1])
+        back = remote(half(x, zi, 1 - yl), gout.at[0:2], ss_p.at[0], rs_p.at[3], partner)
         back.start()
         gout[...] = wg[:, rows(zi), hcols(x, yl)]
         back.wait_send()
+        back_b.wait_send()
         zs(0, half(x, o[0], 0), zh.at[0]).wait_send()
         zs(2, half(x, o[0], 1), zh.at[1]).wait_send()
         by(0, 0, 0, zi + 2, y0).wait_send()
@@ -671,7 +747,8 @@
 
     @pl.when(bad)
     def _():
-        remote(wg.at[:, rows(zi), hcols(x, 1 - yl)], gout, ss_p.at[0], rs_p.at[3], partner).wait_recv()
+        remote(half(x, zi, 1 - yl), gout.at[0:2], ss_p.at[0], rs_p.at[3], partner).wait_recv()
+        remote(bhalf(x, 1 - yl), gout.at[2], ss_p.at[1], rs_p.at[4], partner).wait_recv()
         zs(0, blk(x, o[0]), z1.at[0]).wait_send()
         zs(2, blk(x, o[1]), z1.at[1]).wait_send()
         for q in (0, 1):
@@ -706,17 +783,17 @@
         in_specs=[vm] * 7,
         out_specs=(vm, vm),
         scratch_shapes=[
-            f32(8, 904, TOK), f32(8, 904, TOK), f32(3, 448, 1024), bf16(2, 3, 448, 1024),
-            bf16(2, 2, 256, 448), bf16(2, 2, 448, 1024), f32(8, TOK, 8), f32(4, 2, TOK, 768),
-            f32(4, TOK, 768), f32(3, TOK, 768), f32(4, 2, TOK, 768), bf16(2, 3, 1024, 1024),
-            f32(8, 448, TOK), f32(4, 2, *hlf), f32(4, 2, *full),
+            f32(8, 456, TOK), f32(8, 448, TOK), f32(8, 456, TOK), f32(8, 448, TOK), f32(3, 448, 1024),
+            bf16(2, 3, 448, 1024), bf16(2, 1024, 448), bf16(2, 256, 448), bf16(2, 2, 448, 1024), f32(8, TOK, 8), f32(4, 2, TOK, 768),
+            f32(4, TOK, 768), f32(2, 64, 768), f32(2, TOK, 768), f32(4, 2, TOK, 768), bf16(2, 3, 1024, 1024),
+            f32(4, 2, *hlf), f32(4, 2, *full),
             f32(2, *hlf), f32(2, *full), f32(2, *full), f32(2, *full),
             f32(2, ROWS, 1024), f32(2, ROWS, 1024), f32(2, ROWS, 1024), f32(2, ROWS, 1024),
             f32(2, ROWS, 128), f32(2, ROWS, 256),
             dma((4,)), dma((4,)), dma((2, 2, 2)), dma((2, 2, 2)), dma((2, 2, 2)), dma((4,)),
-            dma((4,)), dma((7,)), dma((7,)), dma((4,)), dma((4,)), dma((4,)), dma((4,)),
+            dma((5,)), dma((7,)), dma((7,)), dma((7,)), dma((7,)), dma((4,)), dma((5,)), dma((4,)), dma((4,)),
             dma((4, 4)), dma((4, 4)),
-            dma((4,)), dma((4,)), dma((3,)), dma((3,)), dma((3,)), dma((3,)), dma((4,)), dma((4,)),
+            dma((2, 4)), dma((2, 4)), dma((2, 4)), dma((2, 4)), dma((4,)), dma((4,)), dma((4,)), dma((4,)),
             dma((4, 2)), dma((4, 2)), dma((4, 2)), dma((4, 2)), dma((7,)), dma((7,)), dma((4,)), dma((4,)),
         ],
         compiler_params=pltpu.CompilerParams(

time: 175 us -> 160 us (0.914); the launches traced: 171 us -> 160 us
  Pallas kernels: 166 us -> 155 us
    pallas_call x1, Pallas kernels: 166 us -> 155 us  [local(): pl.pallas_call(kernel, out_shape=(jax.ShapeDtypeStruct((TOK, 3584), F32),...]
where the time goes in v3:
time: 160 us
  Pallas kernels  155 us (97%)
  local copies, waits for them, and re-layouts  4.4 us (3%)
    pallas_call x1, Pallas kernels, local(): pl.pallas_call(kernel, out_shape=(jax.ShapeDtypeStruct((TOK, 3584), F32),...  155 us

profile of v3, /device:TPU:32, one launch (start us, length us, event | category | flops | bytes accessed | tf_op | source)
XLA Modules:
  0.0 159.8 jit_solution(13172308087601380492)
XLA Ops:
  0.6 154.7 %shard_map.102 = (f32[128,3584]{1,0:T(8,128)}, f32[3,112,128]{2,1,0:T(8,128)}) custom-call(f32[128,3584]{1,0:T(8,128)} %tok.1, f32[128,3584]{1,0:T(8,128)} %cot.1, s32[2,128]{1,0:T(2,128)} %bitcast.8, f32[2,128]{1,0:T(2,128)} %bitcast.9, f32[112,128]{1,0:T(8,128)} %bitcast.5, f32[112,128]{1,0:T(8,128)} %bitcast.6, f32[112,128]{1,0:T(8,128)} %bitcast.7), custom_call_target="tpu_custom_call" | custom-call | flops 20000000000 | bytes 8000000 | tf_op jit(solution)/shard_map/pallas_call | solution.py:780
  155.4 1.5 fusion
  156.9 2.9 %copy.12 = f32[128,3584]{1,0:T(8,128)} copy(f32[128,3584]{1,0:T(8,128)} %get-tuple-element.15) | data formatting | bytes 3670016

commit v4 on v3

--- a/solution.py
+++ b/solution.py
@@ -69,7 +69,7 @@
 
 def kernel(
     tok, cot, route, gate, w0, w1, w2, out, gout,
-    xs, xc, xg, cg, wg, wsp, tsp, csp, ttsp, infot, part, buf, got_h, got, ga, gd, xh, xf, zh, z1, z2, z3,
+    tokv, cotv, xs, xc, xg, cg, wg, wsp, tsp, csp, ttsp, infot, part, buf, got_h, got, ga, gd, xh, xf, zh, z1, z2, z3,
     y0, y1, y2b, y3, yh, yf, ss_bx, rs_bx, ss_bz, rs_bz, rs_by, rs_by2,
     s_l, ss_x, rs_x, ss_xc, rs_xc, ss_p, rs_p, ss_z, rs_z, ss_r, rs_r,
     ss_a, rs_a, ss_b, rs_b, ss_c, rs_c, ss_d, rs_d,
@@ -85,6 +85,10 @@
     xp, xm = dev(x + 1, y, z, c), dev(x - 1, y, z, c)
     partner = dev(x, (y // 2) * 2 + 1 - yl, z, c)
     sib = dev(x, y, z, 1 - c)
+    load_t = pltpu.make_async_copy(tok, tokv, s_l.at[5])
+    load_c = pltpu.make_async_copy(cot, cotv, s_l.at[6])
+    load_t.start()
+    load_c.start()
     greet([dev(x, y + dy, z, c + dc) for dc, dy in OTHERS] + [zp, zm, xp, xm])
 
     def rows(b):
@@ -144,16 +148,13 @@
             cps.append(remote(src.at[y2 * 2 + c2], dst.at[me], ss.at[i], rs.at[i], dev(x, y2, z, c2)))
         return cps
 
-    transpose(tok, xs)
+    load_t.wait()
+    transpose(tokv, xs)
     keep = pltpu.make_async_copy(xs.at[me], xg.at[me], s_l.at[3])
     keep.start()
     tokens_out = group(xs, xg, ss_x, rs_x)
     for cp in tokens_out:
         cp.start()
-    transpose(cot, xc)
-    keep_c = pltpu.make_async_copy(xc.at[me], cg.at[me], s_l.at[4])
-    keep_c.start()
-    cot_out = group(xc, cg, ss_xc, rs_xc)
 
     def member_rows(y2, c2):
         return pl.ds(pl.multiple_of(y2 * 256 + c2 * 128, 128), 128)
@@ -221,6 +222,17 @@
         bx(0, bblk(x)).start()
         bx(1, bblk(x)).start()
         start_x(0, b0)
+
+    load_c.wait()
+    transpose(cotv, xc)
+    keep_c = pltpu.make_async_copy(xc.at[me], cg.at[me], s_l.at[4])
+    keep_c.start()
+    cot_out = group(xc, cg, ss_xc, rs_xc)
+    for cp in cot_out:
+        cp.start()
+
+    @pl.when(good)
+    def _():
         bx(0, bblk(x - 1)).wait_recv()
         bx(2, bhalf(x - 1, 0)).start()
         bx(1, bblk(x + 1)).wait_recv()
@@ -278,11 +290,14 @@
             bz(1, 0, 1 - q, b2).wait_recv()
             bz(1, 1, 1 - q, b2).start()
 
+    keep.wait()
     for cp in tokens_out:
-        cp.wait_send()
-    for cp in cot_out:
-        cp.start()
+        cp.wait_recv()
+    prepare_t(y)
+    prepare_t((y + 1) % 4)
     forward_x(2, b2)
+    prepare_t((y + 2) % 4)
+    prepare_t((y + 3) % 4)
 
     @pl.when(good)
     def _():
@@ -299,11 +314,6 @@
         bz(0, 1, 1, b2).wait_recv()
         bz(1, 1, 0, b3).wait_recv()
 
-    keep.wait()
-    for cp in tokens_out:
-        cp.wait_recv()
-    for i in range(4):
-        prepare_t((y + i) % 4)
     forward_x(3, b3)
     for s, b in enumerate((b0, b1, b2, b3)):
         finish_x(s, b)
@@ -333,6 +343,8 @@
         for cp in shift:
             cp.wait_send()
 
+    for cp in tokens_out:
+        cp.wait_send()
     def split_w(kinds):
         def step(i, _):
             r = pl.ds(pl.multiple_of(i * 32, 32), 32)
@@ -719,7 +731,9 @@
         cp.wait()
     for j in range(28):
         t = jnp.concatenate([cg[m, to : to + n, :] for m, to, frm, n in PIECES[j]], axis=0)
-        out[:, j * 128 : (j + 1) * 128] = t.T
+        tokv[:, j * 128 : (j + 1) * 128] = t.T
+    leave = pltpu.make_async_copy(tokv, out, s_l.at[5])
+    leave.start()
 
     @pl.when(good)
     def _():
@@ -760,6 +774,7 @@
         by(1, 1, q, zi, y2b).wait_send()
     zs(1, blk(x, o[2]), z3.at[0]).wait_send()
     zs(3, blk(x, o[3]), z3.at[1]).wait_send()
+    leave.wait()
     for s in range(4):
         for h in range(2):
             shalf(s, h).wait_send()
@@ -768,6 +783,7 @@
 
 def local(tokens, cotangent, routes, gates, w_gate, w_up, w_down):
     vm = pl.BlockSpec(memory_space=pltpu.VMEM)
+    anyspace = pl.BlockSpec(memory_space=pl.ANY)
     dma = pltpu.SemaphoreType.DMA
     full, hlf = (2, ROWS, 256), (2, ROWS, 128)
 
@@ -780,10 +796,10 @@
     out, gout = pl.pallas_call(
         kernel,
         out_shape=(jax.ShapeDtypeStruct((TOK, 3584), F32), jax.ShapeDtypeStruct((3, ROWS, 128), F32)),
-        in_specs=[vm] * 7,
-        out_specs=(vm, vm),
+        in_specs=[anyspace] * 2 + [vm] * 5,
+        out_specs=(anyspace, vm),
         scratch_shapes=[
-            f32(8, 456, TOK), f32(8, 448, TOK), f32(8, 456, TOK), f32(8, 448, TOK), f32(3, 448, 1024),
+            f32(TOK, 3584), f32(TOK, 3584), f32(8, 456, TOK), f32(8, 448, TOK), f32(8, 456, TOK), f32(8, 448, TOK), f32(3, 448, 1024),
             bf16(2, 3, 448, 1024), bf16(2, 1024, 448), bf16(2, 256, 448), bf16(2, 2, 448, 1024), f32(8, TOK, 8), f32(4, 2, TOK, 768),
             f32(4, TOK, 768), f32(2, 64, 768), f32(2, TOK, 768), f32(4, 2, TOK, 768), bf16(2, 3, 1024, 1024),
             f32(4, 2, *hlf), f32(4, 2, *full),
@@ -791,7 +807,7 @@
             f32(2, ROWS, 1024), f32(2, ROWS, 1024), f32(2, ROWS, 1024), f32(2, ROWS, 1024),
             f32(2, ROWS, 128), f32(2, ROWS, 256),
             dma((4,)), dma((4,)), dma((2, 2, 2)), dma((2, 2, 2)), dma((2, 2, 2)), dma((4,)),
-            dma((5,)), dma((7,)), dma((7,)), dma((7,)), dma((7,)), dma((4,)), dma((5,)), dma((4,)), dma((4,)),
+            dma((7,)), dma((7,)), dma((7,)), dma((7,)), dma((7,)), dma((4,)), dma((5,)), dma((4,)), dma((4,)),
             dma((4, 4)), dma((4, 4)),
             dma((2, 4)), dma((2, 4)), dma((2, 4)), dma((2, 4)), dma((4,)), dma((4,)), dma((4,)), dma((4,)),
             dma((4, 2)), dma((4, 2)), dma((4, 2)), dma((4, 2)), dma((7,)), dma((7,)), dma((4,)), dma((4,)),

time: 160 us -> 158 us (0.988)
  Pallas kernels: 155 us -> 153 us
    pallas_call x1, Pallas kernels: 155 us -> 153 us  [local(): pl.pallas_call(kernel, out_shape=(jax.ShapeDtypeStruct((TOK, 3584), F32),...]
where the time goes in v4:
time: 158 us
  Pallas kernels  153 us (97%)
  local copies, waits for them, and re-layouts  4.4 us (3%)
    pallas_call x1, Pallas kernels, local(): pl.pallas_call(kernel, out_shape=(jax.ShapeDtypeStruct((TOK, 3584), F32),...  153 us

profile of v4, /device:TPU:32, one launch (start us, length us, event | category | flops | bytes accessed | tf_op | source)
XLA Modules:
  0.0 158.0 jit_solution(871923433814087657)
XLA Ops:
  0.6 152.9 %shard_map.102 = (f32[128,3584]{1,0:T(8,128)}, f32[3,112,128]{2,1,0:T(8,128)}) custom-call(f32[128,3584]{1,0:T(8,128)} %tok.1, f32[128,3584]{1,0:T(8,128)} %cot.1, s32[2,128]{1,0:T(2,128)} %bitcast.8, f32[2,128]{1,0:T(2,128)} %bitcast.9, f32[112,128]{1,0:T(8,128)} %bitcast.5, f32[112,128]{1,0:T(8,128)} %bitcast.6, f32[112,128]{1,0:T(8,128)} %bitcast.7), custom_call_target="tpu_custom_call" | custom-call | flops 20000000000 | bytes 8000000 | tf_op jit(solution)/shard_map/pallas_call | solution.py:796
  153.6 1.5 fusion
  155.1 2.9 %copy.12 = f32[128,3584]{1,0:T(8,128)} copy(f32[128,3584]{1,0:T(8,128)} %get-tuple-element.15) | data formatting | bytes 3670016

commit v5 on v4

--- a/solution.py
+++ b/solution.py
@@ -646,7 +646,6 @@
     def bf(h):
         return remote(bblk(x + 1 - 2 * h), yf.at[h], ss_bx.at[2 + h], rs_by2.at[2 + h], xm if h else xp)
 
-    token_grad(0)
     total_x(0)
 
     @pl.when(good)
@@ -661,6 +660,7 @@
         take(1, 1, 0, lo, y2b)
         by(1, 1, 0, lo, y3).start()
 
+    token_grad(0)
     token_grad(1)
 
     @pl.when(bad)

time: 158 us -> 158 us (level)
  no operation moved by 1% of the time
where the time goes in v5:
time: 158 us; the launch traced here: 157 us
  Pallas kernels  152 us (96%)
  local copies, waits for them, and re-layouts  4.4 us (3%)
    pallas_call x1, Pallas kernels, local(): pl.pallas_call(kernel, out_shape=(jax.ShapeDtypeStruct((TOK, 3584), F32),...  152 us

profile of v5, /device:TPU:32, one launch (start us, length us, event | category | flops | bytes accessed | tf_op | source)
XLA Modules:
  0.0 157.4 jit_solution(3665065926914724543)
XLA Ops:
  0.6 152.4 %shard_map.102 = (f32[128,3584]{1,0:T(8,128)}, f32[3,112,128]{2,1,0:T(8,128)}) custom-call(f32[128,3584]{1,0:T(8,128)} %tok.1, f32[128,3584]{1,0:T(8,128)} %cot.1, s32[2,128]{1,0:T(2,128)} %bitcast.8, f32[2,128]{1,0:T(2,128)} %bitcast.9, f32[112,128]{1,0:T(8,128)} %bitcast.5, f32[112,128]{1,0:T(8,128)} %bitcast.6, f32[112,128]{1,0:T(8,128)} %bitcast.7), custom_call_target="tpu_custom_call" | custom-call | flops 20000000000 | bytes 8000000 | tf_op jit(solution)/shard_map/pallas_call | solution.py:796
  153.0 1.5 fusion
  154.6 2.9 %copy.12 = f32[128,3584]{1,0:T(8,128)} copy(f32[128,3584]{1,0:T(8,128)} %get-tuple-element.15) | data formatting | bytes 3670016
